TPU v7x, 32 devices: a whole 2x2x4 slice. The times are simulated.
32 devices in a mesh: groups: 2 (over x), ctx: 16 (over z, y, core).
Axes of the slice: x: 2, y: 2, z: 4, core: 2. Of those that a mesh axis runs over, the one named last changes fastest.
Arguments:
- xbc: bfloat16 [8192, 9216], P(('groups', 'ctx')), parts along dimension 0, may hold values from -35 to 35
- conv_carry: bfloat16 [6, 9216], P('groups'), parts along dimension 0, may hold values from -6 to 6
- conv_weight: float32 [4, 9216], replicated, may hold values from -0.9 to 0.9
- step_size: float32 [8192, 128], P(('groups', 'ctx')), parts along dimension 0, may hold values from 0.01 to 0.1
- decay: float32 [8192, 128], P(('groups', 'ctx')), parts along dimension 0, may hold values from 0.3 to 1
- skip_gain: float32 [128], replicated, may hold values from 0.5 to 1.5
- norm_gain: float32 [8192], replicated, may hold values from 0.5 to 1.5
- init_state: bfloat16 [256, 64, 128], P('groups'), parts along dimension 0, may hold values from -6 to 6
Outputs:
- mixed_out: bfloat16 [8192, 8192], P(('groups', 'ctx')), parts along dimension 0
- final_state: float32 [256, 64, 128], P(('groups', 'ctx')), parts along dimension 0
There are 2 independent parts, one for each index of `groups`. A program takes and returns all parts, laid end to end along the dimension named above; an argument that names none is the same for every part. Nothing has to cross between parts.
All inputs are finite; a program needn't handle non-finite values.
Results may differ from a plain program's by a relative error of at most 0.0048.
Values may be sent and summed in bfloat16 or wider, within the bound.
A program may use at most 256 MiB of HBM per device.

v0:
```python
import jax
import jax.numpy as jnp
from jax import lax
from jax.sharding import PartitionSpec as P

P_SIZE = 64
N = 128
GROUPS = 4
SPAN = 128


def from_behind(value, axis, steps):
    count = lax.axis_size(axis)
    leading, last = (max(0, -steps), min(count, count - steps))
    return lax.ppermute(value, axis, [(source, source + steps) for source in range(leading, last)])


def conv_silu(padded, conv_weight, row_count):
    summed = jnp.zeros((row_count, padded.shape[1]), jnp.float32)
    for offset in range(conv_weight.shape[0]):
        summed = (
            summed + padded[offset : offset + row_count].astype(jnp.float32) * conv_weight[offset]
        )
    return jax.nn.silu(summed).astype(jnp.bfloat16)


def inside(values_part, b_part, c_part, step_part, log_part):
    length, head_count, head_dim = values_part.shape
    groups = b_part.shape[1]
    per_group = head_count // groups
    cum_log = jnp.cumsum(log_part, axis=0)
    scores = jnp.einsum("ign,jgn->gij", c_part, b_part, preferred_element_type=jnp.float32)
    scores = jnp.repeat(scores, per_group, axis=0)
    cum_heads = cum_log.T
    index_of_row = lax.broadcasted_iota(jnp.int32, (length, length), 0)
    col_index = lax.broadcasted_iota(jnp.int32, (length, length), 1)
    lower_mask = (index_of_row >= col_index)[None]
    log_gaps = jnp.where(lower_mask, cum_heads[:, :, None] - cum_heads[:, None, :], 0.0)
    weights = jnp.where(
        lower_mask, scores * jnp.exp(log_gaps) * step_part.T[:, None, :], 0.0
    ).astype(jnp.bfloat16)
    diag_part = jnp.einsum("hij,jhp->ihp", weights, values_part, preferred_element_type=jnp.float32)
    to_end = jnp.exp(cum_log[-1][None, :] - cum_log)
    scaled = (values_part.astype(jnp.float32) * (to_end * step_part)[:, :, None]).astype(
        jnp.bfloat16
    )
    local_state = jnp.einsum(
        "jgkp,jgn->gkpn",
        scaled.reshape(length, groups, per_group, head_dim),
        b_part,
        preferred_element_type=jnp.float32,
    )
    return (diag_part, local_state.reshape(head_count, head_dim, b_part.shape[2]), cum_log)


def carried(carry_state, c_part, cum_log):
    head_count, head_dim, state_dim = carry_state.shape
    groups = c_part.shape[1]
    grouped = carry_state.reshape(groups, head_count // groups, head_dim, state_dim)
    off_part = jnp.einsum(
        "gkpn,ign->igkp", grouped, c_part.astype(jnp.float32), precision=lax.Precision.HIGHEST
    )
    return off_part.reshape(c_part.shape[0], head_count, head_dim) * jnp.exp(cum_log)[:, :, None]


def finish(diag_part, off_part, values_part, skip_gain, norm_gain, groups):
    summed = diag_part + off_part + skip_gain[None, :, None] * values_part.astype(jnp.float32)
    length = summed.shape[0]
    grouped = summed.reshape(length, groups, -1)
    factor = lax.rsqrt(jnp.mean(grouped * grouped, axis=-1, keepdims=True) + 1e-05)
    return ((grouped * factor).reshape(length, -1) * norm_gain[None, :]).astype(jnp.bfloat16)


def shards(xbc, conv_carry, conv_weight, step_size, decay, skip_gain, norm_gain, init_state):
    kernel = conv_weight.shape[0]
    row_count = xbc.shape[0]
    head_count = step_size.shape[1]
    inner_width = head_count * P_SIZE
    blocks = row_count // SPAN
    edge_rows = xbc[row_count - (kernel - 1) :]
    received = from_behind(edge_rows, "ctx", 1)
    position = lax.axis_index("ctx")
    earlier = jnp.where(position == 0, conv_carry, received)
    activated = conv_silu(jnp.concatenate([earlier, xbc], axis=0), conv_weight, row_count)
    values_all = activated[:, :inner_width].reshape(blocks, SPAN, head_count, P_SIZE)
    b_all = activated[:, inner_width : inner_width + GROUPS * N].reshape(blocks, SPAN, GROUPS, N)
    c_all = activated[:, inner_width + GROUPS * N :].reshape(blocks, SPAN, GROUPS, N)
    steps_all = step_size.reshape(blocks, SPAN, head_count)
    logs_all = jnp.log(decay).reshape(blocks, SPAN, head_count)
    diag_all, local_all, cum_all = jax.vmap(inside)(values_all, b_all, c_all, steps_all, logs_all)
    block_logs = cum_all[:, -1, :]

    def advance(carry_state, pieces):
        total_log, local_state = pieces
        return (jnp.exp(total_log)[:, None, None] * carry_state + local_state, carry_state)

    own_state, entering = lax.scan(
        advance, jnp.zeros((head_count, P_SIZE, N), jnp.float32), (block_logs, local_all)
    )
    before_log = jnp.cumsum(block_logs, axis=0) - block_logs
    device_log = jnp.sum(block_logs, axis=0)
    start_state = init_state.astype(jnp.float32)
    head_share = head_count // lax.axis_size("ctx")
    states_in, logs_in = (
        lax.all_to_all(
            own_state[None].astype(jnp.bfloat16), "ctx", split_axis=1, concat_axis=0, tiled=True
        ).astype(jnp.float32),
        lax.all_to_all(
            device_log[None, :, None, None].astype(jnp.bfloat16),
            "ctx",
            split_axis=1,
            concat_axis=0,
            tiled=True,
        ).astype(jnp.float32),
    )
    mine_start = lax.dynamic_slice_in_dim(start_state, position * head_share, head_share, 0)

    def chain_step(state_now, pieces):
        piece_state, piece_log = pieces
        return (jnp.exp(piece_log) * state_now + piece_state, state_now)

    final_state, entering_mine = lax.scan(chain_step, mine_start, (states_in, logs_in))
    returned = lax.all_to_all(entering_mine, "ctx", split_axis=0, concat_axis=1, tiled=True)
    incoming = returned[0]
    block_states = entering + jnp.exp(before_log)[:, :, None, None] * incoming[None]
    off_all = jax.vmap(carried)(block_states, c_all, cum_all)
    mixed_out = finish(
        diag_all.reshape(row_count, head_count, P_SIZE),
        off_all.reshape(row_count, head_count, P_SIZE),
        values_all.reshape(row_count, head_count, P_SIZE),
        skip_gain,
        norm_gain,
        GROUPS,
    )
    return (mixed_out, final_state)


def solution(mesh):
    return jax.shard_map(
        shards,
        mesh=mesh,
        in_specs=(
            P(("groups", "ctx"), None),
            P("groups", None),
            P(),
            P(("groups", "ctx"), None),
            P(("groups", "ctx"), None),
            P(),
            P(),
            P("groups", None, None),
        ),
        out_specs=(P(("groups", "ctx"), None), P(("groups", "ctx"), None, None)),
        check_vma=False,
    )
```

profile of v0, /device:TPU:17, one launch (start us, length us, event | category | flops | bytes accessed | tf_op | source)
XLA Modules:
  0.0 348.0 jit_solution(5774023741636083486)
XLA Ops:
  1.6 3.7 %collective-permute-start = (bf16[3,9216]{1,0:T(4,128)(2,1)S(1)}, bf16[3,9216]{1,0:T(4,128)(2,1)S(1)}, u32[]{:S(2)}, u32[]{:S(2)}) collective-permute-start(bf16[3,9216]{1,0:T(4,128)(2,1)S(1)} %slice.37), channel_id=1, source_target_pairs={{0,1},{1,2},{2,3},{3,4},{4,5},{5,6},{6,7},{7,8},{8,9},{9,10},{10,1... | collective-permute-start | bytes 165896 | tf_op jit(solution)/shard_map/ppermute | solution.py:15
  7.3 5.0 %all-to-all-start = ((bf16[1,128,1,1]{3,2,0,1:T(2,128)(2,1)}), bf16[1,128,1,1]{3,2,0,1:T(2,128)(2,1)S(1)}, u32[]{:S(2)}, u32[]{:S(2)}) async-start(bf16[1,128,1,1]{3,2,0,1:T(2,128)(2,1)} %copy.62), calls=%async_computation | async-start | bytes 131072 | tf_op jit(solution)/shard_map/all_to_all | solution.py:108
  12.3 1.3 fusion.32
  14.9 6.6 %copy.45 = bf16[256,9216]{0,1:T(8,128)(2,1)} copy(bf16[256,9216]{1,0:T(8,128)(2,1)} %param.12) | data formatting | bytes 9437184 | tf_op args[0]
  21.6 1.2 copy.43
  22.9 2.0 copy.44
  24.9 1.9 broadcast_select_fusion
  26.8 1.1 copy-done.4
  27.9 12.7 %multiply_convert_fusion = bf16[256,9216]{0,1:T(8,128)(2,1)S(1)} fusion(bf16[256,9216]{0,1:T(8,128)(2,1)S(1)} %copy-done.4, bf16[3,9216]{0,1:T(8,128)(2,1)S(1)} %broadcast_select_fusion, f32[9216]{0:T(1024)S(1)} %bitcast.111, f32[9216]{0:T(1024)S(1)} %bitcast.112, f32[9216]{0:T(1024)S(1)} %bitcast.110, f32[9216]{0:T(1024)S(1)} %bitcast.109), kind=kLoop, calls=%fused_computation.11 | loop fusion | flops 58982400 | bytes 9639936 | tf_op jit(solution)/shard_map/convert_element_type | solution.py:24
  40.6 5.8 %fusion.30 = (bf16[256,8192]{0,1:T(8,128)(2,1)}, f32[256,8192]{0,1:T(8,128)}) fusion(bf16[256,9216]{0,1:T(8,128)(2,1)S(1)} %multiply_convert_fusion), kind=kLoop, calls=%fused_computation.57 | loop fusion | flops 2097152 | bytes 16777216 | tf_op jit(solution)/shard_map/slice | solution.py:85
  46.5 10.8 %reshape.179 = f32[2,128,4,32,64]{1,0,4,3,2:T(2,128)} reshape(f32[256,8192]{0,1:T(8,128)} %get-tuple-element.122) | data formatting | bytes 16777216 | tf_op jit(solution)/shard_map/vmap()/convert_element_type | solution.py:44
  57.3 10.3 %multiply_convert_fusion.1 = bf16[2,128,4,32,64]{1,0,4,3,2:T(2,128)(2,1)} fusion(f32[2,128,4,32,64]{1,0,4,3,2:T(2,128)} %reshape.179, f32[2,128,4,32]{1,0,3,2:T(2,128)S(1)} %copy.59), kind=kLoop, calls=%fused_computation.23 | loop fusion | flops 4194304 | bytes 12713984 | tf_op jit(solution)/shard_map/vmap()/convert_element_type | solution.py:44
  67.6 6.7 %fusion.17 = f32[2,4,32,64,128]{4,3,2,1,0:T(8,128)} fusion(bf16[2,128,4,32,64]{1,0,4,3,2:T(2,128)(2,1)} %multiply_convert_fusion.1, bf16[2,128,4,128,1]{1,0,3,2,4:T(2,128)(2,1)S(1)} %bitcast.103), kind=kOutput, calls=%fused_computation.34 | convolution fusion | flops 536870912 | bytes 12845056 | tf_op jit(solution)/shard_map/vmap(jgkp,jgn->gkpn)/dot_general | solution.py:47
  74.3 18.0 %while.26 = (s32[]{:T(128)}, f32[128,64,128]{2,1,0:T(8,128)}, f32[2,128,64,128]{3,2,1,0:T(8,128)}, f32[2,128]{1,0:T(2,128)S(1)}, f32[2,128,64,128]{3,2,1,0:T(8,128)}, /*index=5*/s32[]{:T(128)}, s32[]{:T(128)}) while((s32[]{:T(128)}, f32[128,64,128]{2,1,0:T(8,128)}, f32[2,128,64,128]{3,2,1,0:T(8,128)}, f32[2,128]{1,0:T(2,128)S(1)}, ...), condition=%wide.region_2.3_spmd.clone, body=%wide.region_1.2_spmd.clone.sunk | while | flops 4194307 | bytes 54528120 | solution.py:97
  74.3 3.0 bitcast_dynamic-update-slice_fusion.5
  77.2 1.9 copy-done
  79.2 2.5 bitcast_add_fusion.5
  81.7 5.1 %bitcast_dynamic-update-slice_fusion.5 = f32[2,128,64,128]{3,2,1,0:T(8,128)} fusion(f32[2,128,64,128]{3,2,1,0:T(8,128)} %get-tuple-element.203, s32[]{:T(128)} %get-tuple-element.201, f32[128,64,128]{2,1,0:T(8,128)} %get-tuple-element.202, pred[]{:T(512)S(6)} %compare.3), kind=kLoop, calls=%fused_computation.5.clone.1 | loop fusion | flops 1048576 | bytes 8389121 | tf_op jit(solution)/shard_map/while/body/jit(dynamic_update_index_in_dim)/dynamic_update_slice | solution.py:97
  87.5 4.7 %bitcast_add_fusion.5 = f32[128,64,128]{2,1,0:T(8,128)} fusion(f32[2,128,64,128]{3,2,1,0:T(8,128)S(1)} %copy-done, s32[]{:T(128)} %get-tuple-element.201, f32[128,64,128]{2,1,0:T(8,128)} %get-tuple-element.202, f32[128]{0:T(128)S(1)} %fusion.37, pred[]{:T(512)S(6)} %compare.3), kind=kLoop, calls=%fused_computation.6.clone.1 | loop fusion | flops 3145728 | bytes 12583429 | tf_op jit(solution)/shard_map/while/body/eval_jaxpr/add | solution.py:95
  92.2 4.0 %convert_bitcast_fusion = bf16[1,128,64,128]{3,2,0,1:T(8,128)(2,1)} fusion(f32[128,64,128]{2,1,0:T(8,128)} %get-tuple-element.59), kind=kLoop, calls=%fused_computation.39 | loop fusion | flops 1048576 | bytes 6291456 | tf_op jit(solution)/shard_map/convert_element_type | solution.py:106
  96.3 6.0 %all-to-all-start.1 = ((bf16[1,128,64,128]{3,2,0,1:T(8,128)(2,1)}), bf16[1,128,64,128]{3,2,0,1:T(8,128)(2,1)S(1)}, u32[]{:S(2)}, u32[]{:S(2)}) async-start(bf16[1,128,64,128]{3,2,0,1:T(8,128)(2,1)} %convert_bitcast_fusion), calls=%async_computation.1 | async-start | bytes 4194304 | tf_op jit(solution)/shard_map/all_to_all | solution.py:105
  104.3 45.1 %all-to-all-done.1 = bf16[1,128,64,128]{3,2,0,1:T(8,128)(2,1)S(1)} async-done(((bf16[1,128,64,128]{3,2,0,1:T(8,128)(2,1)}), bf16[1,128,64,128]{3,2,0,1:T(8,128)(2,1)S(1)}, u32[]{:S(2)}, u32[]{:S(2)}) %all-to-all-start.1) | async-done | bytes 2097184 | tf_op jit(solution)/shard_map/all_to_all | solution.py:105
  149.4 2.4 convert.3
  151.8 28.9 %while.25 = (s32[]{:T(128)}, f32[8,64,128]{2,1,0:T(8,128)S(1)}, f32[16,8,64,128]{3,2,1,0:T(8,128)}, f32[16,8,1,1]{1,3,2,0:T(1,128)S(1)}, f32[16,8,64,128]{3,2,1,0:T(8,128)}, /*index=5*/s32[]{:T(128)}) while((s32[]{:T(128)}, f32[8,64,128]{2,1,0:T(8,128)S(1)}, f32[16,8,64,128]{3,2,1,0:T(8,128)}, f32[16,8,1,1]{1,3,2,0:T(1,128)S(1)}, ...), condition=%wide.region_6.7_spmd, body=%wide.region_5.6_spmd.sunk | while | flops 131074 | bytes 1311405 | solution.py:122
  152.6 1.1 bitcast_add_fusion.4
  154.4 1.1 bitcast_add_fusion.4
  156.2 1.1 bitcast_add_fusion.4
  158.0 1.1 bitcast_add_fusion.4
  159.8 1.1 bitcast_add_fusion.4
  161.6 1.1 bitcast_add_fusion.4
  163.4 1.1 bitcast_add_fusion.4
  165.2 1.1 bitcast_add_fusion.4
  167.0 1.1 bitcast_add_fusion.4
  168.9 1.1 bitcast_add_fusion.4
  170.7 1.1 bitcast_add_fusion.4
  180.8 5.2 %all-to-all-start.2 = ((f32[16,8,64,128]{3,2,1,0:T(8,128)}), f32[16,8,64,128]{3,2,1,0:T(8,128)}, u32[]{:S(2)}, u32[]{:S(2)}) async-start(f32[16,8,64,128]{3,2,1,0:T(8,128)} %get-tuple-element.60), calls=%async_computation.2 | async-start | bytes 8388608 | tf_op jit(solution)/shard_map/all_to_all | solution.py:123
  190.0 6.9 %reshape.167 = bf16[2,128,128,64]{1,0,3,2:T(2,128)(2,1)} reshape(bf16[256,8192]{0,1:T(8,128)(2,1)} %get-tuple-element.121) | data formatting | bytes 8388608 | tf_op jit(solution)/shard_map/reshape | solution.py:85
  196.9 1.1 fusion.26
  198.0 80.2 %all-to-all-done.2 = f32[16,8,64,128]{3,2,1,0:T(8,128)} async-done(((f32[16,8,64,128]{3,2,1,0:T(8,128)}), f32[16,8,64,128]{3,2,1,0:T(8,128)}, u32[]{:S(2)}, u32[]{:S(2)}) %all-to-all-start.2) | async-done | bytes 4194336 | tf_op jit(solution)/shard_map/all_to_all | solution.py:123
  278.2 5.1 %multiply_add_fusion = f32[2,128,64,128]{3,2,1,0:T(8,128)S(1)} fusion(f32[2,128,64,128]{3,2,1,0:T(8,128)} %get-tuple-element.58, f32[128,64,128]{2,1,0:T(8,128)} %bitcast.22, f32[2,128]{1,0:T(2,128)S(1)} %subtract_exponential_fusion), kind=kLoop, calls=%fused_computation.22 | loop fusion | flops 4194304 | bytes 20972544 | tf_op jit(solution)/shard_map/add | solution.py:125
  283.3 4.5 %fusion.24 = f32[2,4,128,32,64]{2,4,3,1,0:T(8,128)S(1)} fusion(f32[2,4,32,64,128]{4,3,2,1,0:T(8,128)S(1)} %bitcast.99, bf16[2,128,4,128,1]{1,0,3,2,4:T(2,128)(2,1)S(1)} %bitcast.102), kind=kOutput, calls=%fused_computation.41 | convolution fusion | flops 3221225472 | bytes 17039360 | tf_op jit(solution)/shard_map/vmap(gkpn,ign->igkp)/dot_general | solution.py:60
  287.9 8.1 %broadcast_in_dim.52 = f32[2,4,32,128,128]{4,3,2,1,0:T(8,128)} broadcast(f32[2,4,128,128]{3,2,1,0:T(8,128)S(1)} %copy-done.6), dimensions={0,1,3,4} | broadcast | bytes 17301504 | tf_op jit(solution)/shard_map/vmap()/broadcast_in_dim | solution.py:33
  296.0 1.3 copy-done.2
  297.2 13.2 %multiply_reduce_fusion = (f32[2,128,128]{1,2,0:T(8,128)S(1)}, f32[2,128,128,64]{1,3,2,0:T(8,128)S(1)}) fusion(f32[2,128,128,64]{1,3,2,0:T(8,128)S(1)} %bitcast.95, f32[128]{0:T(128)S(1)} %copy-done.11, f32[2,128,128]{1,2,0:T(8,128)} %copy.67, bf16[2,128,128,64]{1,0,3,2:T(2,128)(2,1)S(1)} %copy-done.5, f32[2,128,128,128]{3,2,1,0:T(8,128)} %bitcast.100, ...), kind=kOutput, calls=%fused_computation.21 | convolution fusion | flops 576684032 | bytes 38289920 | tf_op jit(solution)/shard_map/vmap(hij,jhp->ihp)/dot_general | solution.py:42
  310.4 7.7 %copy.55 = f32[2,128,128,64]{1,0,3,2:T(2,128)} copy(f32[2,128,128,64]{1,3,2,0:T(8,128)S(1)} %get-tuple-element.131) | data formatting | bytes 16777216 | tf_op jit(solution)/shard_map/vmap(hij,jhp->ihp)/transpose | solution.py:42
  318.4 14.5 %copy.65 = f32[2,128,4,32,64]{1,0,4,3,2:T(2,128)S(1)} copy(f32[2,128,4,32,64]{1,4,3,2,0:T(8,128)} %bitcast.96) | data formatting | bytes 16777216 | tf_op jit(solution)/shard_map/vmap(gkpn,ign->igkp)/transpose | solution.py:60
  332.9 8.7 %fusion.9 = bf16[256,8192]{0,1:T(8,128)(2,1)} fusion(f32[1024,8,2,128]{3,2,1,0:T(2,128)S(1)} %bitcast.98, f32[1024,8,2,128]{3,2,1,0:T(2,128)} %bitcast.97, f32[8192]{0:T(1024)S(1)} %copy-done.10, f32[256,4]{0,1:T(4,128)S(1)} %add_rsqrt_fusion, f32[8192]{0:T(1024)S(1)} %mul.196, f32[256,128]{0,1:T(8,128)S(1)} %copy-done.7, bf16[256,9216]{0,1:T(8,128)(2,1)} %copy-done.1), kind=kLoop, calls=%fused_computation.20 | loop fusion | flops 16777216 | bytes 25366528 | tf_op jit(solution)/shard_map/convert_element_type | solution.py:71
  341.7 6.3 %copy.70 = bf16[256,8192]{1,0:T(8,128)(2,1)} copy(bf16[256,8192]{0,1:T(8,128)(2,1)} %fusion.9) | data formatting | bytes 8388608
  (99 shorter events, 28.5 us)
Async XLA Ops:
  0.6 20.9 %copy-start.9 = (bf16[3,9216]{1,0:T(4,128)(2,1)S(1)}, bf16[3,9216]{1,0:T(4,128)(2,1)}, u32[]{:S(2)}) copy-start(bf16[3,9216]{1,0:T(4,128)(2,1)} %param.13) | copy-start | bytes 165892
  1.6 21.2 %collective-permute-start = (bf16[3,9216]{1,0:T(4,128)(2,1)S(1)}, bf16[3,9216]{1,0:T(4,128)(2,1)S(1)}, u32[]{:S(2)}, u32[]{:S(2)}) collective-permute-start(bf16[3,9216]{1,0:T(4,128)(2,1)S(1)} %slice.37), channel_id=1, source_target_pairs={{0,1},{1,2},{2,3},{3,4},{4,5},{5,6},{6,7},{7,8},{8,9},{9,10},{10,1... | collective-permute-start | bytes 165896 | tf_op jit(solution)/shard_map/ppermute | solution.py:15
  7.3 89.0 %all-to-all-start = ((bf16[1,128,1,1]{3,2,0,1:T(2,128)(2,1)}), bf16[1,128,1,1]{3,2,0,1:T(2,128)(2,1)S(1)}, u32[]{:S(2)}, u32[]{:S(2)}) async-start(bf16[1,128,1,1]{3,2,0,1:T(2,128)(2,1)} %copy.62), calls=%async_computation | async-start | bytes 131072 | tf_op jit(solution)/shard_map/all_to_all | solution.py:108
  24.9 3.0 copy-start.4
  40.6 5.9 %copy-start.1 = (bf16[256,9216]{0,1:T(8,128)(2,1)}, bf16[256,9216]{0,1:T(8,128)(2,1)S(1)}, u32[]{:S(2)}) copy-start(bf16[256,9216]{0,1:T(8,128)(2,1)S(1)} %multiply_convert_fusion) | copy-start | bytes 14155780
  74.3 4.9 %copy-start = (f32[2,128,64,128]{3,2,1,0:T(8,128)S(1)}, f32[2,128,64,128]{3,2,1,0:T(8,128)}, u32[]{:S(2)}) copy-start(f32[2,128,64,128]{3,2,1,0:T(8,128)} %get-tuple-element.212) | copy-start | bytes 25165828 | tf_op jit(solution)/shard_map/while
  81.7 5.8 %copy-start = (f32[2,128,64,128]{3,2,1,0:T(8,128)S(1)}, f32[2,128,64,128]{3,2,1,0:T(8,128)}, u32[]{:S(2)}) copy-start(f32[2,128,64,128]{3,2,1,0:T(8,128)} %get-tuple-element.212) | copy-start | bytes 25165828 | tf_op jit(solution)/shard_map/while
  96.3 53.2 %all-to-all-start.1 = ((bf16[1,128,64,128]{3,2,0,1:T(8,128)(2,1)}), bf16[1,128,64,128]{3,2,0,1:T(8,128)(2,1)S(1)}, u32[]{:S(2)}, u32[]{:S(2)}) async-start(bf16[1,128,64,128]{3,2,0,1:T(8,128)(2,1)} %convert_bitcast_fusion), calls=%async_computation.1 | async-start | bytes 4194304 | tf_op jit(solution)/shard_map/all_to_all | solution.py:105
  151.8 35.7 %copy-start.8 = (f32[256,128]{1,0:T(8,128)S(1)}, f32[256,128]{1,0:T(8,128)}, u32[]{:S(2)}) copy-start(f32[256,128]{1,0:T(8,128)} %param.15) | copy-start | bytes 393220
  151.8 37.2 %copy-start.11 = (f32[128]{0:T(128)S(1)}, f32[128]{0:T(128)}, u32[]{:S(2)}) copy-start(f32[128]{0:T(128)} %param.17) | copy-start | bytes 1540
  180.8 16.1 %copy-start.3 = (f32[8,64,128]{2,1,0:T(8,128)}, f32[8,64,128]{2,1,0:T(8,128)S(1)}, u32[]{:S(2)}) copy-start(f32[8,64,128]{2,1,0:T(8,128)S(1)} %get-tuple-element.98) | copy-start | bytes 786436
  180.8 97.4 %all-to-all-start.2 = ((f32[16,8,64,128]{3,2,1,0:T(8,128)}), f32[16,8,64,128]{3,2,1,0:T(8,128)}, u32[]{:S(2)}, u32[]{:S(2)}) async-start(f32[16,8,64,128]{3,2,1,0:T(8,128)} %get-tuple-element.60), calls=%async_computation.2 | async-start | bytes 8388608 | tf_op jit(solution)/shard_map/all_to_all | solution.py:123
  283.3 4.5 %copy-start.6 = (f32[2,4,128,128]{3,2,1,0:T(8,128)S(1)}, f32[2,4,128,128]{3,2,1,0:T(8,128)}, u32[]{:S(2)}) copy-start(f32[2,4,128,128]{3,2,1,0:T(8,128)} %fusion.26) | copy-start | bytes 1572868
  287.8 9.4 %copy-start.2 = (f32[2,4,128,32,64]{2,4,3,1,0:T(8,128)}, f32[2,4,128,32,64]{2,4,3,1,0:T(8,128)S(1)}, u32[]{:S(2)}) copy-start(f32[2,4,128,32,64]{2,4,3,1,0:T(8,128)S(1)} %fusion.24) | copy-start | bytes 25165828
  287.9 9.4 %copy-start.5 = (bf16[2,128,128,64]{1,0,3,2:T(2,128)(2,1)S(1)}, bf16[2,128,128,64]{1,0,3,2:T(2,128)(2,1)}, u32[]{:S(2)}) copy-start(bf16[2,128,128,64]{1,0,3,2:T(2,128)(2,1)} %reshape.167) | copy-start | bytes 12582916
  318.4 14.5 %copy-start.7 = (f32[256,128]{0,1:T(8,128)S(1)}, f32[256,128]{0,1:T(8,128)}, u32[]{:S(2)}) copy-start(f32[256,128]{0,1:T(8,128)} %copy.66) | copy-start | bytes 393220
  318.4 14.5 %copy-start.10 = (f32[8192]{0:T(1024)S(1)}, f32[8192]{0:T(1024)}, u32[]{:S(2)}) copy-start(f32[8192]{0:T(1024)} %param.18) | copy-start | bytes 98308
where the time goes:
time: 350 us; the launch traced here: 348 us
  waiting for transfers between devices  125 us (36%)
  local copies, waits for them, and re-layouts  89.9 us (26%)
  other arithmetic  86.1 us (25%)
  matrix products  25.5 us (7%)
  starting transfers between devices  19.9 us (6%)
    all_to_all x1, waiting for transfers between devices, shards(): lax.all_to_all(entering_mine, 'ctx', split_axis=0, concat_axis=1, tiled=T...  80.2 us
    all_to_all x1, waiting for transfers between devices, shards(): lax.all_to_all(own_state[None].astype(jnp.bfloat16), 'ctx', split_axis=1,...  45.1 us
    unnamed x26, local copies, waits for them, and re-layouts  17.6 us
    add x16, other arithmetic, chain_step(): return (jnp.exp(piece_log) * state_now + piece_state, state_now)  16.9 us
    transpose x1, local copies, waits for them, and re-layouts, carried(): jnp.einsum('gkpn,ign->igkp', grouped, c_part.astype(jnp.float32), precisi...  14.5 us
    dot_general x1, matrix products, inside(): jnp.einsum('hij,jhp->ihp', weights, values_part, preferred_element_type=j...  13.2 us
    convert_element_type x1, other arithmetic, conv_silu(): return jax.nn.silu(summed).astype(jnp.bfloat16)  12.7 us
    dynamic_update_slice x16, local copies, waits for them, and re-layouts, shards(): lax.scan(chain_step, mine_start, (states_in, logs_in))  11.6 us
  transfers between devices with their start and end apart: 4, of which 2 were waited for; matrix products, arithmetic and copies ran while one was open for 28% of the time, Pallas kernels for 0%

commit v1 on v0

v1 whole, which is shorter than its diff:
```python
import jax
import jax.numpy as jnp
from jax import lax
from jax.experimental import pallas as pl
from jax.experimental.pallas import tpu as pltpu
from jax.sharding import PartitionSpec as P

P_SIZE = 64
N = 128
GROUPS = 4
LANES = 128
F32 = jnp.float32
BF16 = jnp.bfloat16
VMEM_LIMIT = 48 * 1024 * 1024


def params():
    return pltpu.CompilerParams(
        dimension_semantics=("arbitrary",), vmem_limit_bytes=VMEM_LIMIT
    )


def split_bf16(value):
    high = value.astype(BF16)
    low = (value - high.astype(F32)).astype(BF16)
    return high, low


def conv_columns(x_ref, early_ref, weight_ref, out_ref, padded, rows):
    def column(index, _):
        at = pl.ds(pl.multiple_of(index * LANES, LANES), LANES)
        padded[0:8, :] = early_ref[:, at]
        padded[8 : 8 + rows, :] = x_ref[:, at].astype(F32)
        taps = weight_ref[:, at]
        summed = taps[0:1] * padded[5 : 5 + rows, :]
        for tap in range(1, 4):
            summed = summed + taps[tap : tap + 1] * padded[5 + tap : 5 + tap + rows, :]
        half = 0.5 * summed
        out_ref[:, at] = (half * jnp.tanh(half) + half).astype(BF16)
        return 0

    lax.fori_loop(0, x_ref.shape[1] // LANES, column, 0)


def conv_kernel(
    xv, xb, xc, ev, eb, ec, wv, wb, wc, factor, expand, act_v, act_b, act_c, state, padded
):
    rows = xv.shape[0]
    conv_columns(xv, ev, wv, act_v, padded, rows)
    conv_columns(xb, eb, wb, act_b, padded, rows)
    conv_columns(xc, ec, wc, act_c, padded, rows)
    b_turned = act_b[...].astype(F32).T.astype(BF16)
    dests, _, share = state.shape
    for dest in range(dests):
        at = slice(dest * share, (dest + 1) * share)
        wide = jnp.dot(factor[0], expand[:, at], preferred_element_type=F32)
        scaled = (act_v[:, at].astype(F32) * wide).astype(BF16)
        state[dest] = jnp.dot(b_turned, scaled, preferred_element_type=F32).astype(BF16)


def diag_kernel(act_v, act_b, act_c, cum_rows, shifted, skip, partial):
    rows = act_v.shape[0]
    half = rows // 2
    heads = cum_rows.shape[2]
    scores = lax.dot_general(
        act_c[...], act_b[...], (((1,), (1,)), ((), ())), preferred_element_type=F32
    )
    row_index = lax.broadcasted_iota(jnp.int32, (half, half), 0)
    col_index = lax.broadcasted_iota(jnp.int32, (half, half), 1)
    lower = row_index >= col_index
    first_lanes = lax.broadcasted_iota(jnp.int32, (half, 2 * P_SIZE), 1) < P_SIZE
    cum = cum_rows[0]
    for pair in range(heads // 2):
        at = slice(pair * 2 * P_SIZE, (pair + 1) * 2 * P_SIZE)
        values = act_v[:, at]
        tops, lows = [], []
        for head in (2 * pair, 2 * pair + 1):
            own = cum[:, head : head + 1]
            other = shifted[head : head + 1, :]
            top = jnp.where(lower, own[:half] - other[:, :half], -1e30)
            w_top = (scores[:half, :half] * jnp.exp2(top)).astype(BF16)
            left = own[half:] - other[:, :half]
            w_left = (scores[half:, :half] * jnp.exp2(left)).astype(BF16)
            right = jnp.where(lower, own[half:] - other[:, half:], -1e30)
            w_right = (scores[half:, half:] * jnp.exp2(right)).astype(BF16)
            tops.append(jnp.dot(w_top, values[:half], preferred_element_type=F32))
            w_low = jnp.concatenate([w_left, w_right], axis=1)
            lows.append(jnp.dot(w_low, values, preferred_element_type=F32))
        gain = skip[:, at]
        wide = values.astype(F32)
        partial[:half, at] = (
            jnp.where(first_lanes, tops[0], tops[1]) + gain * wide[:half]
        ).astype(BF16)
        partial[half:, at] = (
            jnp.where(first_lanes, lows[0], lows[1]) + gain * wide[half:]
        ).astype(BF16)


def chain_kernel(states, decays, start, entering, final):
    def step(index, now):
        entering[index] = now.astype(BF16)
        return decays[index] * now + states[index].astype(F32)

    final[...] = lax.fori_loop(0, states.shape[0], step, start[...])


def finish_kernel(partial, act_c, incoming, grown, expand, gain, out, summed):
    dests, _, share = incoming.shape
    squares = jnp.zeros((partial.shape[0], 1), F32)
    for dest in range(dests):
        at = slice(dest * share, (dest + 1) * share)
        wide = jnp.dot(grown[0], expand[:, at], preferred_element_type=F32)
        off = jnp.dot(act_c[...], incoming[dest], preferred_element_type=F32)
        total = partial[:, at].astype(F32) + wide * off
        summed[:, at] = total
        squares = squares + jnp.sum(total * total, axis=1, keepdims=True)
    factor = lax.rsqrt(squares * (1.0 / out.shape[1]) + 1e-05)
    for dest in range(dests):
        at = slice(dest * share, (dest + 1) * share)
        out[:, at] = (summed[:, at] * factor * gain[:, at]).astype(BF16)


def shards(xbc, conv_carry, conv_weight, step_size, decay, skip_gain, norm_gain, init_state):
    taps, channels = conv_weight.shape
    rows = xbc.shape[0]
    heads = step_size.shape[1]
    inner = heads * P_SIZE
    count = lax.axis_size("ctx")
    position = lax.axis_index("ctx")
    share = inner // count
    head_share = heads // count
    width = inner // GROUPS
    per_group = heads // GROUPS
    dests = width // share

    edge = xbc[rows - (taps - 1) :]
    received = lax.ppermute(edge, "ctx", [(s, s + 1) for s in range(count - 1)])
    earlier = jnp.where(position == 0, conv_carry, received).astype(F32)
    earlier = jnp.pad(earlier, ((8 - (taps - 1), 0), (0, 0)))

    logs = jnp.log2(decay)
    lower = jnp.tril(jnp.ones((rows, rows), F32))
    cum = jnp.dot(lower, logs, precision=lax.Precision.HIGHEST)
    total = cum[-1]

    def by_group(value):
        return value.reshape(rows, GROUPS, -1).transpose(1, 0, 2)

    def doubled(value):
        high, low = split_bf16(by_group(value))
        return jnp.concatenate([high, low], axis=2)

    factor = doubled(jnp.exp2(total - cum) * step_size)
    grown = doubled(jnp.exp2(cum))
    shifted = (cum - jnp.log2(step_size)).T
    spread = jnp.repeat(jnp.eye(per_group, dtype=BF16), P_SIZE, axis=1)
    expand = jnp.concatenate([spread, spread], axis=0)

    totals = lax.all_to_all(
        total.reshape(count, head_share), "ctx", split_axis=0, concat_axis=0, tiled=True
    )
    decays = jnp.repeat(jnp.exp2(totals), P_SIZE, axis=1)[:, None, :]

    def wide(height):
        return pl.BlockSpec((height, width), lambda g: (0, g))

    def thin(height, first):
        return pl.BlockSpec((height, N), lambda g: (0, first + g))

    def per(*shape):
        return pl.BlockSpec((1,) + shape, lambda g: (g, 0, 0))

    whole_expand = pl.BlockSpec((2 * per_group, width), lambda g: (0, 0))
    piece = pl.BlockSpec((dests, N, share), lambda g: (g, 0, 0))
    b_first, c_first = inner // N, inner // N + GROUPS
    act_v, act_b, act_c, own = pl.pallas_call(
        conv_kernel,
        grid=(GROUPS,),
        in_specs=[
            wide(rows), thin(rows, b_first), thin(rows, c_first),
            wide(8), thin(8, b_first), thin(8, c_first),
            wide(taps), thin(taps, b_first), thin(taps, c_first),
            per(rows, 2 * per_group), whole_expand,
        ],
        out_specs=[wide(rows), thin(rows, 0), thin(rows, 0), piece],
        out_shape=[
            jax.ShapeDtypeStruct((rows, inner), BF16),
            jax.ShapeDtypeStruct((rows, GROUPS * N), BF16),
            jax.ShapeDtypeStruct((rows, GROUPS * N), BF16),
            jax.ShapeDtypeStruct((count, N, share), BF16),
        ],
        scratch_shapes=[pltpu.VMEM((8 + rows, LANES), F32)],
        compiler_params=params(),
        name="conv_state",
    )(xbc, xbc, xbc, earlier, earlier, earlier, conv_weight, conv_weight, conv_weight, factor, expand)

    states = lax.all_to_all(own, "ctx", split_axis=0, concat_axis=0, tiled=True)

    partial = pl.pallas_call(
        diag_kernel,
        grid=(GROUPS,),
        in_specs=[
            wide(rows), thin(rows, 0), thin(rows, 0), per(rows, per_group),
            pl.BlockSpec((per_group, rows), lambda g: (g, 0)), wide(1),
        ],
        out_specs=wide(rows),
        out_shape=jax.ShapeDtypeStruct((rows, inner), BF16),
        compiler_params=params(),
        cost_estimate=pl.CostEstimate(
            flops=heads * rows * rows * P_SIZE * 16,
            bytes_accessed=rows * inner * 4,
            transcendentals=heads * rows * rows,
        ),
        name="diag",
    )(act_v, act_b, act_c, by_group(cum), shifted, jnp.repeat(skip_gain, P_SIZE)[None])

    start = lax.dynamic_slice_in_dim(init_state, position * head_share, head_share, 0)
    start = start.astype(F32).reshape(share, N).T
    entering, final = pl.pallas_call(
        chain_kernel,
        grid=(share // LANES,),
        in_specs=[
            pl.BlockSpec((count, N, LANES), lambda i: (0, 0, i)),
            pl.BlockSpec((count, 1, LANES), lambda i: (0, 0, i)),
            pl.BlockSpec((N, LANES), lambda i: (0, i)),
        ],
        out_specs=[
            pl.BlockSpec((count, N, LANES), lambda i: (0, 0, i)),
            pl.BlockSpec((N, LANES), lambda i: (0, i)),
        ],
        out_shape=[
            jax.ShapeDtypeStruct((count, N, share), BF16),
            jax.ShapeDtypeStruct((N, share), F32),
        ],
        compiler_params=params(),
        name="chain",
    )(states, decays, start)
    final_state = final.T.reshape(head_share, P_SIZE, N)

    incoming = lax.all_to_all(entering, "ctx", split_axis=0, concat_axis=0, tiled=True)

    mixed_out = pl.pallas_call(
        finish_kernel,
        grid=(GROUPS,),
        in_specs=[
            wide(rows), thin(rows, 0), piece, per(rows, 2 * per_group), whole_expand, wide(1),
        ],
        out_specs=wide(rows),
        out_shape=jax.ShapeDtypeStruct((rows, inner), BF16),
        scratch_shapes=[pltpu.VMEM((rows, width), F32)],
        compiler_params=params(),
        name="finish",
    )(partial, act_c, incoming, grown, expand, norm_gain[None])
    return (mixed_out, final_state)


def solution(mesh):
    return jax.shard_map(
        shards,
        mesh=mesh,
        in_specs=(
            P(("groups", "ctx"), None),
            P("groups", None),
            P(),
            P(("groups", "ctx"), None),
            P(("groups", "ctx"), None),
            P(),
            P(),
            P("groups", None, None),
        ),
        out_specs=(P(("groups", "ctx"), None), P(("groups", "ctx"), None, None)),
        check_vma=False,
    )
```

time: 350 us -> 153 us (0.44)
  other arithmetic: 86.1 us -> 4.86 us
  local copies, waits for them, and re-layouts: 89.9 us -> 19.4 us
  waiting for transfers between devices: 125 us -> 75.1 us
  Pallas kernels: 0 us -> 30.8 us
  matrix products: 25.5 us -> 0.4 us
    all_to_all x3, waiting for transfers between devices: 125 us -> 75.1 us  [the longest x1 46 us: shards(): states = lax.all_to_all(own, 'ctx', split_axis=0, concat_axis=0, tiled=True)]
    convert_element_type x7 -> x3, other arithmetic: 40 us -> 1.9 us  [the longest x2 1.89 us: split_bf16(): low = (value - high.astype(F32)).astype(BF16)]
    pallas_call x0 -> x4, Pallas kernels: none -> 30.8 us  [the longest x1 12 us: shards(): pl.pallas_call(conv_kernel, grid=(GROUPS,), in_specs=[wide(rows), thin(ro...]
    add x19 -> x0, other arithmetic: 29.3 us -> none  [the longest x16 16.9 us: chain_step(): return (jnp.exp(piece_log) * state_now + piece_state, state_now)]
    dot_general x4 -> x1, matrix products: 25.5 us -> 0.4 us  [shards(): cum = jnp.dot(lower, logs, precision=lax.Precision.HIGHEST)]
    transpose x4 -> x2, local copies, waits for them, and re-layouts: 23.7 us -> 1.91 us  [the longest x1 1.78 us: shards(): final_state = final.T.reshape(head_share, P_SIZE, N)]
    convert_element_type x3 -> x0, local copies, waits for them, and re-layouts: 11.6 us -> none  [the longest x1 10.8 us: inside(): values_part.astype(jnp.float32) * (to_end * step_part)[:, :, None]]
    dynamic_update_slice x16 -> x0, local copies, waits for them, and re-layouts: 11.6 us -> none  [shards(): lax.scan(chain_step, mine_start, (states_in, logs_in))]
  transfers between devices with their start and end apart: 4 -> 4, of which waited for: 2 -> 2; matrix products, arithmetic and copies ran while one was open for 28% -> 9% of each run, Pallas kernels for 0% -> 14%
where the time goes in v1:
time: 153 us; the launch traced here: 151 us
  waiting for transfers between devices  75.1 us (49%)
  Pallas kernels  30.8 us (20%)
  starting transfers between devices  20 us (13%)
  local copies, waits for them, and re-layouts  19.4 us (13%)
  other arithmetic  4.86 us (3%)
    all_to_all x1, waiting for transfers between devices, shards(): states = lax.all_to_all(own, 'ctx', split_axis=0, concat_axis=0, tiled=True)  46 us
    all_to_all x1, waiting for transfers between devices, shards(): lax.all_to_all(entering, 'ctx', split_axis=0, concat_axis=0, tiled=True)  29.1 us
    pallas_call x1, Pallas kernels, shards(): pl.pallas_call(conv_kernel, grid=(GROUPS,), in_specs=[wide(rows), thin(ro...  12 us
    unnamed x25, local copies, waits for them, and re-layouts  10.5 us
    pallas_call x1, Pallas kernels, shards(): pl.pallas_call(diag_kernel, grid=(GROUPS,), in_specs=[wide(rows), thin(ro...  8.73 us
    pallas_call x1, Pallas kernels, shards(): pl.pallas_call(finish_kernel, grid=(GROUPS,), in_specs=[wide(rows), thin(...  7.04 us
    all_to_all x1, starting transfers between devices, shards(): states = lax.all_to_all(own, 'ctx', split_axis=0, concat_axis=0, tiled=True)  6.02 us
    all_to_all x1, starting transfers between devices, shards(): lax.all_to_all(entering, 'ctx', split_axis=0, concat_axis=0, tiled=True)  5.32 us
  transfers between devices with their start and end apart: 4, of which 2 were waited for; matrix products, arithmetic and copies ran while one was open for 9% of the time, Pallas kernels for 14%

profile of v1, /device:TPU:17, one launch (start us, length us, event | category | flops | bytes accessed | tf_op | source)
XLA Modules:
  0.0 151.5 jit_solution(16363625933240312787)
XLA Ops:
  0.6 0.0 copy-start
  0.6 1.7 %slice.6 = bf16[3,9216]{1,0:T(4,128)(2,1)} slice(bf16[256,9216]{1,0:T(8,128)(2,1)} %xc.1), slice={[253:256], [0:9216]} | slice | bytes 110592 | tf_op jit(solution)/shard_map/slice | solution.py:136
  2.4 3.7 %collective-permute-start = (bf16[3,9216]{1,0:T(4,128)(2,1)}, bf16[3,9216]{1,0:T(4,128)(2,1)}, u32[]{:S(2)}, u32[]{:S(2)}) collective-permute-start(bf16[3,9216]{1,0:T(4,128)(2,1)} %slice.6), channel_id=1, source_target_pairs={{0,1},{1,2},{2,3},{3,4},{4,5},{5,6},{6,7},{7,8},{8,9},{9,10},{10,1... | collective-permute-start | bytes 165896 | tf_op jit(solution)/shard_map/ppermute | solution.py:137
  6.1 1.0 copy.38
  7.1 0.4 fusion.2
  7.5 0.2 slice_reduce_fusion
  7.7 0.7 all_to_all.13
  8.4 5.0 %all-to-all-start.1 = ((f32[16,1,8]{2,1,0:T(1,128)}), f32[16,1,8]{2,1,0:T(1,128)}, u32[]{:S(2)}, u32[]{:S(2)}) async-start(f32[16,1,8]{2,1,0:T(1,128)} %bitcast.5), calls=%async_computation.1 | async-start | bytes 16384 | tf_op jit(solution)/shard_map/all_to_all | solution.py:159
  13.4 1.0 copy.39
  14.4 0.7 subtract_bitcast_fusion
  15.1 0.2 copy.40
  15.3 0.8 fusion.1
  16.1 0.2 broadcast_in_dim.23
  16.3 0.3 reshape.32
  16.6 1.1 pad_maximum_fusion.factor
  17.7 0.0 collective-permute-done
  17.7 0.9 broadcast_select_fusion
  18.7 0.0 copy-done.4
  18.7 12.0 %conv_state.1 = (bf16[256,8192]{1,0:T(8,128)(2,1)}, bf16[256,512]{1,0:T(8,128)(2,1)S(1)}, bf16[256,512]{1,0:T(8,128)(2,1)S(1)}, bf16[16,128,512]{2,1,0:T(8,128)(2,1)S(1)}) custom-call(bf16[256,9216]{1,0:T(8,128)(2,1)} %xc.1, bf16[256,9216]{1,0:T(8,128)(2,1)} %xc.1, bf16[256,9216]{1,0:T(8,128)(2,1)} %xc.1, f32[8,9216]{1,0:T(8,128)S(1)} %pad_convert_fusion.ev.eb.ec, ...), custom_call_target="tpu_custom_call" | custom-call | tf_op jit(solution)/shard_map/conv_state/pallas_call | solution.py:176
  30.7 0.0 copy-start.2
  30.7 1.3 copy-done.2
  32.0 0.0 all-to-all-done.1
  32.0 0.7 copy-done.8
  32.7 6.0 %all-to-all-start = ((bf16[16,128,512]{2,1,0:T(8,128)(2,1)}), bf16[16,128,512]{2,1,0:T(8,128)(2,1)}, u32[]{:S(2)}, u32[]{:S(2)}) async-start(bf16[16,128,512]{2,1,0:T(8,128)(2,1)} %copy-done.2), calls=%async_computation | async-start | bytes 4194304 | tf_op jit(solution)/shard_map/all_to_all | solution.py:197
  38.8 0.1 copy.46
  39.0 0.8 copy.44
  39.7 0.1 copy.45
  39.8 0.1 broadcast_in_dim.25
  39.9 0.1 broadcast_in_dim_reshape.7.decays
  40.0 46.0 %all-to-all-done.states = bf16[16,128,512]{2,1,0:T(8,128)(2,1)} async-done(((bf16[16,128,512]{2,1,0:T(8,128)(2,1)}), bf16[16,128,512]{2,1,0:T(8,128)(2,1)}, u32[]{:S(2)}, u32[]{:S(2)}) %all-to-all-start) | async-done | bytes 2097184 | tf_op jit(solution)/shard_map/all_to_all | solution.py:197
  86.0 3.0 %chain.1 = (bf16[16,128,512]{2,1,0:T(8,128)(2,1)S(1)}, f32[128,512]{1,0:T(8,128)S(1)}) custom-call(bf16[16,128,512]{2,1,0:T(8,128)(2,1)} %all-to-all-done.states, f32[16,1,512]{2,1,0:T(1,128)S(1)} %broadcast_in_dim_reshape.7.decays, f32[128,512]{1,0:T(8,128)S(1)} %bitcast.28), custom_call_target="tpu_custom_call" | custom-call | tf_op jit(solution)/shard_map/chain/pallas_call | solution.py:219
  89.0 1.3 copy-done.3
  90.4 0.7 copy-done.5
  91.1 5.3 %all-to-all-start.2 = ((bf16[16,128,512]{2,1,0:T(8,128)(2,1)}), bf16[16,128,512]{2,1,0:T(8,128)(2,1)}, u32[]{:S(2)}, u32[]{:S(2)}) async-start(bf16[16,128,512]{2,1,0:T(8,128)(2,1)} %copy-done.3), calls=%async_computation.2 | async-start | bytes 4194304 | tf_op jit(solution)/shard_map/all_to_all | solution.py:240
  96.4 0.2 copy.41
  96.6 0.7 broadcast_in_dim.24
  97.4 0.7 broadcast_in_dim_reshape.6.skip
  98.1 1.0 copy.47
  99.1 1.1 fusion
  100.2 0.1 pad_maximum_fusion.1.grown
  100.4 0.7 copy-done.7
  101.1 0.9 copy-done.9
  102.1 8.7 %diag.1.partial = bf16[256,8192]{1,0:T(8,128)(2,1)S(1)} custom-call(bf16[256,8192]{1,0:T(8,128)(2,1)} %get-tuple-element.8.act_v, bf16[256,512]{1,0:T(8,128)(2,1)S(1)} %copy-done.9, bf16[256,512]{1,0:T(8,128)(2,1)S(1)} %get-tuple-element.10.act_c, f32[4,256,32]{2,1,0:T(8,128)S(1)} %bitcast.29, f32[128,256]{1,0:T(8,128)S(1)} %get-tuple-element.20.shifted, ...), custom_call_target="tpu_custom_call" | custom-call | flops 8589934592 | bytes 8388608 | tf_op jit(solution)/shard_map/diag/pallas_call | solution.py:199
  110.8 1.9 %copy-done.1 = bf16[256,8192]{1,0:T(8,128)(2,1)} copy-done((bf16[256,8192]{1,0:T(8,128)(2,1)}, bf16[256,8192]{1,0:T(8,128)(2,1)S(1)}, u32[]{:S(2)}) %copy-start.1) | copy-done | bytes 4194328
  112.7 1.8 %copy.48 = f32[512,128]{1,0:T(8,128)} copy(f32[512,128]{0,1:T(8,128)} %bitcast.30) | data formatting | bytes 524288 | tf_op jit(solution)/shard_map/transpose | solution.py:238
  114.5 29.1 %all-to-all-done.2.incoming = bf16[16,128,512]{2,1,0:T(8,128)(2,1)} async-done(((bf16[16,128,512]{2,1,0:T(8,128)(2,1)}), bf16[16,128,512]{2,1,0:T(8,128)(2,1)}, u32[]{:S(2)}, u32[]{:S(2)}) %all-to-all-start.2) | async-done | bytes 2097184 | tf_op jit(solution)/shard_map/all_to_all | solution.py:240
  143.7 0.8 copy-done.6
  144.4 7.0 %finish.1 = bf16[256,8192]{1,0:T(8,128)(2,1)} custom-call(bf16[256,8192]{1,0:T(8,128)(2,1)} %copy-done.1, bf16[256,512]{1,0:T(8,128)(2,1)S(1)} %get-tuple-element.10.act_c, bf16[16,128,512]{2,1,0:T(8,128)(2,1)} %all-to-all-done.2.incoming, bf16[4,256,64]{2,1,0:T(8,128)(2,1)S(1)} %pad_maximum_fusion.1.grown, ...), custom_call_target="tpu_custom_call" | custom-call | tf_op jit(solution)/shard_map/finish/pallas_call | solution.py:242
  (18 shorter events, 0.1 us)
Async XLA Ops:
  0.6 38.1 %copy-start = (bf16[128,64,128]{2,1,0:T(8,128)(2,1)S(1)}, bf16[128,64,128]{2,1,0:T(8,128)(2,1)}, u32[]{:S(2)}) copy-start(bf16[128,64,128]{2,1,0:T(8,128)(2,1)} %param.15) | copy-start | bytes 6291460
  2.4 15.3 %collective-permute-start = (bf16[3,9216]{1,0:T(4,128)(2,1)}, bf16[3,9216]{1,0:T(4,128)(2,1)}, u32[]{:S(2)}, u32[]{:S(2)}) collective-permute-start(bf16[3,9216]{1,0:T(4,128)(2,1)} %slice.6), channel_id=1, source_target_pairs={{0,1},{1,2},{2,3},{3,4},{4,5},{5,6},{6,7},{7,8},{8,9},{9,10},{10,1... | collective-permute-start | bytes 165896 | tf_op jit(solution)/shard_map/ppermute | solution.py:137
  8.4 23.7 %all-to-all-start.1 = ((f32[16,1,8]{2,1,0:T(1,128)}), f32[16,1,8]{2,1,0:T(1,128)}, u32[]{:S(2)}, u32[]{:S(2)}) async-start(f32[16,1,8]{2,1,0:T(1,128)} %bitcast.5), calls=%async_computation.1 | async-start | bytes 16384 | tf_op jit(solution)/shard_map/all_to_all | solution.py:159
  15.1 3.6 %copy-start.4 = (f32[4,9216]{1,0:T(4,128)S(1)}, f32[4,9216]{1,0:T(4,128)}, u32[]{:S(2)}) copy-start(f32[4,9216]{1,0:T(4,128)} %wc.1) | copy-start | bytes 442372
  30.7 1.3 copy-start.2
  32.0 0.7 copy-start.8
  32.7 53.3 %all-to-all-start = ((bf16[16,128,512]{2,1,0:T(8,128)(2,1)}), bf16[16,128,512]{2,1,0:T(8,128)(2,1)}, u32[]{:S(2)}, u32[]{:S(2)}) async-start(bf16[16,128,512]{2,1,0:T(8,128)(2,1)} %copy-done.2), calls=%async_computation | async-start | bytes 4194304 | tf_op jit(solution)/shard_map/all_to_all | solution.py:197
  89.0 1.4 copy-start.3
  90.4 0.7 copy-start.5
  91.1 7.0 %copy-start.10 = (f32[256,128]{0,1:T(8,128)S(1)}, f32[256,128]{0,1:T(8,128)}, u32[]{:S(2)}) copy-start(f32[256,128]{0,1:T(8,128)} %get-tuple-element.22) | copy-start | bytes 393220
  91.1 52.6 %all-to-all-start.2 = ((bf16[16,128,512]{2,1,0:T(8,128)(2,1)}), bf16[16,128,512]{2,1,0:T(8,128)(2,1)}, u32[]{:S(2)}, u32[]{:S(2)}) async-start(bf16[16,128,512]{2,1,0:T(8,128)(2,1)} %copy-done.3), calls=%async_computation.2 | async-start | bytes 4194304 | tf_op jit(solution)/shard_map/all_to_all | solution.py:240
  100.3 0.8 copy-start.7
  101.1 0.9 copy-start.9
  110.8 1.9 %copy-start.1 = (bf16[256,8192]{1,0:T(8,128)(2,1)}, bf16[256,8192]{1,0:T(8,128)(2,1)S(1)}, u32[]{:S(2)}) copy-start(bf16[256,8192]{1,0:T(8,128)(2,1)S(1)} %diag.1.partial) | copy-start | bytes 12582916
  143.7 0.8 copy-start.6

commit v2 on v1

--- a/solution.py
+++ b/solution.py
@@ -1,3 +1,5 @@
+import functools
+
 import jax
 import jax.numpy as jnp
 from jax import lax
@@ -50,12 +52,13 @@
     conv_columns(xb, eb, wb, act_b, padded, rows)
     conv_columns(xc, ec, wc, act_c, padded, rows)
     b_turned = act_b[...].astype(F32).T.astype(BF16)
-    dests, _, share = state.shape
+    share = state.shape[-1]
+    dests = xv.shape[1] // share
     for dest in range(dests):
         at = slice(dest * share, (dest + 1) * share)
         wide = jnp.dot(factor[0], expand[:, at], preferred_element_type=F32)
         scaled = (act_v[:, at].astype(F32) * wide).astype(BF16)
-        state[dest] = jnp.dot(b_turned, scaled, preferred_element_type=F32).astype(BF16)
+        state[dest % 2, dest // 2 % 2, dest // 4] = jnp.dot(b_turned, scaled, preferred_element_type=F32).astype(BF16)
 
 
 def diag_kernel(act_v, act_b, act_c, cum_rows, shifted, skip, partial):
@@ -96,21 +99,158 @@
         ).astype(BF16)
 
 
-def chain_kernel(states, decays, start, entering, final):
-    def step(index, now):
-        entering[index] = now.astype(BF16)
-        return decays[index] * now + states[index].astype(F32)
-
-    final[...] = lax.fori_loop(0, states.shape[0], step, start[...])
+def scan_kernel(
+    planes, own, decays, start, incoming, final,
+    cores, sent, kept, chips, plane_out, plane_in, enter, entered, back, mixed, handed,
+    core_send, core_recv, chip_send, chip_recv, out_send, out_recv,
+    in_send, in_recv, back_send, back_recv, hand_send, hand_recv,
+):
+    position = lax.axis_index("ctx")
+    z, y, c = position // 4, (position // 2) % 2, position % 2
+    core_peer = position + 1 - 2 * c
+    chip_peer = position + 2 - 4 * y
+    away = [(z + step) % planes for step in range(planes)]
+    order = list(range(1, planes)) + [0]
+    first_core = c == 0
+    first_chip = y == 0
+
+    def copy(source, target, send, recv, device):
+        return pltpu.make_async_remote_copy(
+            src_ref=source, dst_ref=target, send_sem=send, recv_sem=recv,
+            device_id={"ctx": device}, device_id_type=pl.DeviceIdType.MESH,
+        )
+
+    barrier = pltpu.get_barrier_semaphore()
+    friends = [core_peer, chip_peer] + [away[step] * 4 + y * 2 + c for step in range(1, planes)]
+    for friend in friends:
+        pl.semaphore_signal(
+            barrier, inc=1, device_id={"ctx": friend}, device_id_type=pl.DeviceIdType.MESH
+        )
+    pl.semaphore_wait(barrier, len(friends))
+
+    pending = []
+    sides = (1 - y, y)
+    swaps = []
+    for turn, side in enumerate(sides):
+        swap = copy(
+            own.at[1 - c, side], cores.at[side], core_send.at[turn], core_recv.at[turn], core_peer
+        )
+        swap.start()
+        swaps.append(swap)
+    pending += swaps
+
+    def core_states(side, plane):
+        here, there = own[c, side, plane].astype(F32), cores[side, plane].astype(F32)
+        return jnp.where(first_core, here, there), jnp.where(first_core, there, here)
+
+    def chip_state(side, plane):
+        earlier, later = core_states(side, plane)
+        return decays[side * planes + plane] * earlier + later
+
+    swaps[0].wait_recv()
+    chip_copies = {}
+    for step in order:
+        plane = away[step]
+        sent[plane] = chip_state(1 - y, plane).astype(BF16)
+        chip_copies[step] = copy(
+            sent.at[plane], chips.at[plane], chip_send.at[step], chip_recv.at[step], chip_peer
+        )
+        chip_copies[step].start()
+        pending.append(chip_copies[step])
+    swaps[1].wait_recv()
+    for step in order:
+        kept[away[step]] = chip_state(y, away[step]).astype(BF16)
+
+    def chip_states(plane):
+        here, there = kept[plane].astype(F32), chips[plane].astype(F32)
+        return jnp.where(first_chip, here, there), jnp.where(first_chip, there, here)
+
+    out_copies = {}
+    for step in order:
+        plane = away[step]
+        chip_copies[step].wait_recv()
+        earlier, later = chip_states(plane)
+        both = (decays[4 * planes + plane] * earlier + later).astype(BF16)
+        if step == 0:
+            plane_in[plane] = both
+        else:
+            plane_out[plane] = both
+            out_copies[step] = copy(
+                plane_out.at[plane], plane_in.at[z], out_send.at[step], out_recv.at[step],
+                plane * 4 + y * 2 + c,
+            )
+            out_copies[step].start()
+            pending.append(out_copies[step])
+    for step in range(1, planes):
+        out_copies[step].wait_recv()
+
+    now = start[...]
+    for plane in range(planes):
+        enter[plane] = now.astype(BF16)
+        now = decays[6 * planes + plane] * now + plane_in[plane].astype(F32)
+    final[...] = now
+    in_copies = {}
+    for step in range(1, planes):
+        plane = away[step]
+        in_copies[step] = copy(
+            enter.at[plane], entered.at[z], in_send.at[step], in_recv.at[step],
+            plane * 4 + y * 2 + c,
+        )
+        in_copies[step].start()
+        pending.append(in_copies[step])
+
+    hands = []
+
+    def to_cores(side, plane, state, slot):
+        earlier, _ = core_states(side, plane)
+        later = decays[2 * planes + side * planes + plane] * state + earlier
+        incoming[c, side, plane] = jnp.where(first_core, state, later).astype(BF16)
+        handed[side, plane] = jnp.where(first_core, later, state).astype(BF16)
+        hand = copy(
+            handed.at[side, plane], incoming.at[c, side, plane],
+            hand_send.at[slot], hand_recv.at[slot], core_peer,
+        )
+        hand.start()
+        hands.append(hand)
+
+    back_copies = {}
+    receive_order = [0] + list(range(1, planes))
+    for step in receive_order:
+        plane = (z + planes - step) % planes
+        if step == 0:
+            state = enter[plane].astype(F32)
+        else:
+            in_copies[step].wait_recv()
+            state = entered[plane].astype(F32)
+        earlier, _ = chip_states(plane)
+        later = decays[5 * planes + plane] * state + earlier
+        back[plane] = jnp.where(first_chip, later, state).astype(BF16)
+        back_copies[step] = copy(
+            back.at[plane], mixed.at[plane], back_send.at[step], back_recv.at[step], chip_peer
+        )
+        back_copies[step].start()
+        pending.append(back_copies[step])
+        to_cores(y, plane, jnp.where(first_chip, state, later), step)
+    for step in receive_order:
+        plane = (z + planes - step) % planes
+        back_copies[step].wait_recv()
+        to_cores(1 - y, plane, mixed[plane].astype(F32), planes + step)
+    for hand in hands:
+        hand.wait_recv()
+    for item in pending + hands:
+        item.wait_send()
 
 
 def finish_kernel(partial, act_c, incoming, grown, expand, gain, out, summed):
-    dests, _, share = incoming.shape
+    share = incoming.shape[-1]
+    dests = out.shape[1] // share
     squares = jnp.zeros((partial.shape[0], 1), F32)
     for dest in range(dests):
         at = slice(dest * share, (dest + 1) * share)
         wide = jnp.dot(grown[0], expand[:, at], preferred_element_type=F32)
-        off = jnp.dot(act_c[...], incoming[dest], preferred_element_type=F32)
+        off = jnp.dot(
+            act_c[...], incoming[dest % 2, dest // 2 % 2, dest // 4], preferred_element_type=F32
+        )
         total = partial[:, at].astype(F32) + wide * off
         summed[:, at] = total
         squares = squares + jnp.sum(total * total, axis=1, keepdims=True)
@@ -156,10 +296,19 @@
     spread = jnp.repeat(jnp.eye(per_group, dtype=BF16), P_SIZE, axis=1)
     expand = jnp.concatenate([spread, spread], axis=0)
 
-    totals = lax.all_to_all(
-        total.reshape(count, head_share), "ctx", split_axis=0, concat_axis=0, tiled=True
-    )
-    decays = jnp.repeat(jnp.exp2(totals), P_SIZE, axis=1)[:, None, :]
+    planes = count // 4
+    at_z, at_y, at_c = position // 4, (position // 2) % 2, position % 2
+    every = lax.all_gather(total, "ctx").reshape(planes, 2, 2, planes, 2, 2, head_share)
+    every = every[:, :, :, :, :, at_c].transpose(0, 1, 2, 4, 3, 5)
+    plane_now = every[at_z]
+    pieces = [
+        plane_now[at_y, 1].reshape(2 * planes, head_share),
+        plane_now[at_y, 0].reshape(2 * planes, head_share),
+        plane_now[1].sum(0)[at_y],
+        plane_now[0].sum(0)[at_y],
+        every.sum((1, 2))[:, at_y, at_z],
+    ]
+    decays = jnp.repeat(jnp.exp2(jnp.concatenate(pieces, axis=0)), P_SIZE, axis=1)[:, None, :]
 
     def wide(height):
         return pl.BlockSpec((height, width), lambda g: (0, g))
@@ -171,7 +320,7 @@
         return pl.BlockSpec((1,) + shape, lambda g: (g, 0, 0))
 
     whole_expand = pl.BlockSpec((2 * per_group, width), lambda g: (0, 0))
-    piece = pl.BlockSpec((dests, N, share), lambda g: (g, 0, 0))
+    piece = pl.BlockSpec((2, 2, dests // 4, N, share), lambda g: (0, 0, g, 0, 0))
     b_first, c_first = inner // N, inner // N + GROUPS
     act_v, act_b, act_c, own = pl.pallas_call(
         conv_kernel,
@@ -187,14 +336,12 @@
             jax.ShapeDtypeStruct((rows, inner), BF16),
             jax.ShapeDtypeStruct((rows, GROUPS * N), BF16),
             jax.ShapeDtypeStruct((rows, GROUPS * N), BF16),
-            jax.ShapeDtypeStruct((count, N, share), BF16),
+            jax.ShapeDtypeStruct((2, 2, planes, N, share), BF16),
         ],
         scratch_shapes=[pltpu.VMEM((8 + rows, LANES), F32)],
         compiler_params=params(),
         name="conv_state",
     )(xbc, xbc, xbc, earlier, earlier, earlier, conv_weight, conv_weight, conv_weight, factor, expand)
-
-    states = lax.all_to_all(own, "ctx", split_axis=0, concat_axis=0, tiled=True)
 
     partial = pl.pallas_call(
         diag_kernel,
@@ -216,28 +363,27 @@
 
     start = lax.dynamic_slice_in_dim(init_state, position * head_share, head_share, 0)
     start = start.astype(F32).reshape(share, N).T
-    entering, final = pl.pallas_call(
-        chain_kernel,
-        grid=(share // LANES,),
-        in_specs=[
-            pl.BlockSpec((count, N, LANES), lambda i: (0, 0, i)),
-            pl.BlockSpec((count, 1, LANES), lambda i: (0, 0, i)),
-            pl.BlockSpec((N, LANES), lambda i: (0, i)),
-        ],
-        out_specs=[
-            pl.BlockSpec((count, N, LANES), lambda i: (0, 0, i)),
-            pl.BlockSpec((N, LANES), lambda i: (0, i)),
-        ],
+    vmem = pl.BlockSpec(memory_space=pltpu.VMEM)
+    line = pltpu.VMEM((planes, N, share), BF16)
+    square = pltpu.VMEM((2, planes, N, share), BF16)
+    turns = pltpu.SemaphoreType.DMA((planes,))
+    incoming, final = pl.pallas_call(
+        functools.partial(scan_kernel, planes),
+        in_specs=[vmem] * 3,
+        out_specs=[vmem] * 2,
         out_shape=[
-            jax.ShapeDtypeStruct((count, N, share), BF16),
+            jax.ShapeDtypeStruct((2, 2, planes, N, share), BF16),
             jax.ShapeDtypeStruct((N, share), F32),
         ],
-        compiler_params=params(),
-        name="chain",
-    )(states, decays, start)
+        scratch_shapes=[square] + [line] * 9 + [square]
+        + [pltpu.SemaphoreType.DMA((2,))] * 2 + [turns] * 8
+        + [pltpu.SemaphoreType.DMA((2 * planes,))] * 2,
+        compiler_params=pltpu.CompilerParams(
+            collective_id=0, has_side_effects=True, vmem_limit_bytes=VMEM_LIMIT
+        ),
+        name="scan_devices",
+    )(own, decays, start)
     final_state = final.T.reshape(head_share, P_SIZE, N)
-
-    incoming = lax.all_to_all(entering, "ctx", split_axis=0, concat_axis=0, tiled=True)
 
     mixed_out = pl.pallas_call(
         finish_kernel,

time: 153 us -> 124 us (0.81)
  waiting for transfers between devices: 75.1 us -> 0.01 us
  Pallas kernels: 30.8 us -> 76.3 us
  starting transfers between devices: 20 us -> 3.7 us
  blocking collectives: 0 us -> 14.8 us
  local copies, waits for them, and re-layouts: 19.4 us -> 22.2 us
    all_to_all x3 -> x0, waiting for transfers between devices: 75.1 us -> none  [the longest x1 46 us: shards(): states = lax.all_to_all(own, 'ctx', split_axis=0, concat_axis=0, tiled=True)]
    pallas_call x1, Pallas kernels: 3.02 us -> 48.5 us  [shards(): pl.pallas_call(functools.partial(scan_kernel, planes), in_specs=[vmem] *...]
    all_to_all x3 -> x0, starting transfers between devices: 16.3 us -> none  [the longest x1 6.02 us: shards(): states = lax.all_to_all(own, 'ctx', split_axis=0, concat_axis=0, tiled=True)]
    all_gather x0 -> x1, blocking collectives: none -> 14.8 us  [shards(): lax.all_gather(total, 'ctx').reshape(planes, 2, 2, planes, 2, 2, head_share)]
    reshape x3, local copies, waits for them, and re-layouts: 1.38 us -> 3.2 us  [by_group(): return value.reshape(rows, GROUPS, -1).transpose(1, 0, 2)]
    convert_element_type x2, other arithmetic: 1.89 us -> 0.14 us  [split_bf16(): low = (value - high.astype(F32)).astype(BF16)]
    unnamed x25 -> x31, local copies, waits for them, and re-layouts: 10.5 us -> 9.69 us
  transfers between devices with their start and end apart: 4 -> 1, of which waited for: 2 -> 0; matrix products, arithmetic and copies ran while one was open for 9% -> 13% of each run, Pallas kernels for 14% -> 0%
where the time goes in v2:
time: 124 us; the launch traced here: 123 us
  Pallas kernels  76.3 us (62%)
  local copies, waits for them, and re-layouts  22.2 us (18%)
  blocking collectives  14.8 us (12%)
  other arithmetic  4.95 us (4%)
  starting transfers between devices  3.7 us (3%)
    pallas_call x1, Pallas kernels, shards(): pl.pallas_call(functools.partial(scan_kernel, planes), in_specs=[vmem] *...  48.5 us
    all_gather x1, blocking collectives, shards(): lax.all_gather(total, 'ctx').reshape(planes, 2, 2, planes, 2, 2, head_share)  14.8 us
    pallas_call x1, Pallas kernels, shards(): pl.pallas_call(conv_kernel, grid=(GROUPS,), in_specs=[wide(rows), thin(ro...  12.1 us
    unnamed x31, local copies, waits for them, and re-layouts  9.69 us
    pallas_call x1, Pallas kernels, shards(): pl.pallas_call(diag_kernel, grid=(GROUPS,), in_specs=[wide(rows), thin(ro...  8.88 us
    pallas_call x1, Pallas kernels, shards(): pl.pallas_call(finish_kernel, grid=(GROUPS,), in_specs=[wide(rows), thin(...  6.77 us
    ppermute x1, starting transfers between devices, shards(): received = lax.ppermute(edge, 'ctx', [(s, s + 1) for s in range(count - 1)])  3.7 us
    reshape x3, local copies, waits for them, and re-layouts, by_group(): return value.reshape(rows, GROUPS, -1).transpose(1, 0, 2)  3.2 us
  transfers between devices with their start and end apart: 1, of which 0 were waited for; matrix products, arithmetic and copies ran while one was open for 13% of the time, Pallas kernels for 0%

profile of v2, /device:TPU:17, one launch (start us, length us, event | category | flops | bytes accessed | tf_op | source)
XLA Modules:
  0.0 123.4 jit_solution(2579771284413992834)
XLA Ops:
  0.6 1.7 %slice.14 = bf16[3,9216]{1,0:T(4,128)(2,1)} slice(bf16[256,9216]{1,0:T(8,128)(2,1)} %xc.1), slice={[253:256], [0:9216]} | slice | bytes 110592 | tf_op jit(solution)/shard_map/slice | solution.py:276
  2.4 3.7 %collective-permute-start = (bf16[3,9216]{1,0:T(4,128)(2,1)}, bf16[3,9216]{1,0:T(4,128)(2,1)}, u32[]{:S(2)}, u32[]{:S(2)}) collective-permute-start(bf16[3,9216]{1,0:T(4,128)(2,1)} %slice.14), channel_id=1, source_target_pairs={{0,1},{1,2},{2,3},{3,4},{4,5},{5,6},{6,7},{7,8},{8,9},{9,10},{10,1... | collective-permute-start | bytes 165896 | tf_op jit(solution)/shard_map/ppermute | solution.py:277
  6.1 0.6 fusion.9
  6.7 1.0 copy.49
  7.7 0.4 fusion.2
  8.1 1.0 copy.50
  9.2 0.2 slice_reduce_fusion
  9.4 0.8 subtract_bitcast_fusion
  10.1 0.2 copy.51
  10.3 0.1 fusion.1
  10.4 0.9 broadcast_in_dim.23
  11.4 0.3 reshape.48
  11.7 14.8 %all-gather = f32[16,1,128]{2,1,0:T(1,128)S(1)} all-gather(f32[1,1,128]{2,1,0:T(1,128)} %bitcast.60), channel_id=1, replica_groups=mesh['groups'=2,'ctx'=16] {'ctx'}, dimensions={0}, use_global_device_ids=true | all-gather | bytes 8704 | tf_op jit(solution)/shard_map/all_gather | solution.py:301
  26.5 0.5 broadcast.26
  27.0 0.7 reduce.10
  27.7 0.2 reshape.50
  28.0 0.1 dynamic-slice_reduce_fusion
  28.2 0.1 copy.59
  28.3 0.1 copy.60
  28.4 0.1 copy.61
  28.5 0.1 copy.62
  28.6 0.1 concatenate.14
  28.7 0.6 multiply_exponential_fusion.1
  29.3 0.7 bitcast_convert_fusion.2
  30.0 1.1 copy.65
  31.1 0.1 fusion
  31.2 0.1 pad_maximum_fusion.factor
  31.4 0.1 pad_maximum_fusion.1.grown
  31.5 1.9 %copy.52 = f32[256,4,32]{2,0,1:T(8,128)} copy(f32[256,4,32]{0,2,1:T(8,128)} %bitcast.48) | data formatting | bytes 262144 | tf_op jit(solution)/shard_map/reshape | solution.py:287
  33.4 0.7 broadcast_in_dim.24
  34.2 0.7 broadcast_in_dim_reshape.6.skip
  34.9 0.8 copy.63
  35.7 0.1 broadcast_in_dim.25
  35.8 0.7 broadcast_in_dim_reshape.7.decays
  36.5 1.1 copy.64
  37.6 0.9 broadcast_select_fusion
  38.6 12.1 %conv_state.1 = (bf16[256,8192]{1,0:T(8,128)(2,1)}, bf16[256,512]{1,0:T(8,128)(2,1)S(1)}, bf16[256,512]{1,0:T(8,128)(2,1)S(1)}, bf16[2,2,4,128,512]{4,3,2,1,0:T(8,128)(2,1)S(1)}) custom-call(bf16[256,9216]{1,0:T(8,128)(2,1)} %xc.1, bf16[256,9216]{1,0:T(8,128)(2,1)} %xc.1, bf16[256,9216]{1,0:T(8,128)(2,1)} %xc.1, f32[8,9216]{1,0:T(8,128)S(1)} %pad_convert_fusion.ev.eb.ec, ...), custom_call_target="tpu_custom_call" | custom-call | tf_op jit(solution)/shard_map/conv_state/pallas_call | solution.py:325
  50.8 0.7 copy-done.10
  51.5 48.5 %scan_devices.1 = (bf16[2,2,4,128,512]{4,3,2,1,0:T(8,128)(2,1)S(1)}, f32[128,512]{1,0:T(8,128)S(1)}) custom-call(bf16[2,2,4,128,512]{4,3,2,1,0:T(8,128)(2,1)S(1)} %get-tuple-element.11.own, f32[28,1,512]{2,1,0:T(1,128)S(1)} %copy-done.6, f32[128,512]{1,0:T(8,128)S(1)} %bitcast.44), custom_call_target="tpu_custom_call" | custom-call | tf_op jit(solution)/shard_map/scan_devices/pallas_call | solution.py:370
  100.0 1.3 %copy-done.2 = bf16[2,2,4,128,512]{4,3,2,1,0:T(8,128)(2,1)} copy-done((bf16[2,2,4,128,512]{4,3,2,1,0:T(8,128)(2,1)}, bf16[2,2,4,128,512]{4,3,2,1,0:T(8,128)(2,1)S(1)}, u32[]{:S(2)}) %copy-start.2) | copy-done | bytes 2097176
  101.3 0.8 copy.66
  102.1 1.0 copy-done.5
  103.2 0.9 copy-done.7
  104.1 0.8 copy-done.9
  104.8 0.9 copy-done.11
  105.8 8.9 %diag.1.partial = bf16[256,8192]{1,0:T(8,128)(2,1)S(1)} custom-call(bf16[256,8192]{1,0:T(8,128)(2,1)} %get-tuple-element.8.act_v, bf16[256,512]{1,0:T(8,128)(2,1)S(1)} %copy-done.11, bf16[256,512]{1,0:T(8,128)(2,1)S(1)} %get-tuple-element.10.act_c, f32[4,256,32]{2,1,0:T(8,128)S(1)} %bitcast.45, f32[128,256]{1,0:T(8,128)S(1)} %copy-done.7, ...), custom_call_target="tpu_custom_call" | custom-call | flops 8589934592 | bytes 8388608 | tf_op jit(solution)/shard_map/diag/pallas_call | solution.py:346
  114.7 1.9 %copy-done.1 = bf16[256,8192]{1,0:T(8,128)(2,1)} copy-done((bf16[256,8192]{1,0:T(8,128)(2,1)}, bf16[256,8192]{1,0:T(8,128)(2,1)S(1)}, u32[]{:S(2)}) %copy-start.1) | copy-done | bytes 4194328
  116.6 6.8 %finish.1 = bf16[256,8192]{1,0:T(8,128)(2,1)} custom-call(bf16[256,8192]{1,0:T(8,128)(2,1)} %copy-done.1, bf16[256,512]{1,0:T(8,128)(2,1)S(1)} %get-tuple-element.10.act_c, bf16[2,2,4,128,512]{4,3,2,1,0:T(8,128)(2,1)S(1)} %copy-done.3, bf16[4,256,64]{2,1,0:T(8,128)(2,1)S(1)} %pad_maximum_fusion.1.grown, ...), custom_call_target="tpu_custom_call" | custom-call | tf_op jit(solution)/shard_map/finish/pallas_call | solution.py:388
  (34 shorter events, 0.3 us)
Async XLA Ops:
  0.6 28.7 %copy-start = (bf16[128,64,128]{2,1,0:T(8,128)(2,1)S(1)}, bf16[128,64,128]{2,1,0:T(8,128)(2,1)}, u32[]{:S(2)}) copy-start(bf16[128,64,128]{2,1,0:T(8,128)(2,1)} %param.15) | copy-start | bytes 6291460
  2.4 35.2 %collective-permute-start = (bf16[3,9216]{1,0:T(4,128)(2,1)}, bf16[3,9216]{1,0:T(4,128)(2,1)}, u32[]{:S(2)}, u32[]{:S(2)}) collective-permute-start(bf16[3,9216]{1,0:T(4,128)(2,1)} %slice.14), channel_id=1, source_target_pairs={{0,1},{1,2},{2,3},{3,4},{4,5},{5,6},{6,7},{7,8},{8,9},{9,10},{10,1... | collective-permute-start | bytes 165896 | tf_op jit(solution)/shard_map/ppermute | solution.py:277
  8.1 2.2 %copy-start.12 = (f32[256,128]{0,1:T(8,128)}, f32[256,128]{0,1:T(8,128)S(1)}, u32[]{:S(2)}) copy-start(f32[256,128]{0,1:T(8,128)S(1)} %fusion.2) | copy-start | bytes 393220
  9.3 1.0 copy-start.13
  10.4 28.2 %copy-start.4 = (f32[4,9216]{1,0:T(4,128)S(1)}, f32[4,9216]{1,0:T(4,128)}, u32[]{:S(2)}) copy-start(f32[4,9216]{1,0:T(4,128)} %wc.1) | copy-start | bytes 442372
  38.6 12.9 %copy-start.6 = (f32[28,1,512]{2,1,0:T(1,128)S(1)}, f32[28,1,512]{2,1,0:T(1,128)}, u32[]{:S(2)}) copy-start(f32[28,1,512]{2,1,0:T(1,128)} %broadcast_in_dim_reshape.7.decays) | copy-start | bytes 172036
  50.8 0.7 copy-start.10
  99.9 1.3 %copy-start.2 = (bf16[2,2,4,128,512]{4,3,2,1,0:T(8,128)(2,1)}, bf16[2,2,4,128,512]{4,3,2,1,0:T(8,128)(2,1)S(1)}, u32[]{:S(2)}) copy-start(bf16[2,2,4,128,512]{4,3,2,1,0:T(8,128)(2,1)S(1)} %get-tuple-element.12.incoming) | copy-start | bytes 6291460
  102.1 1.0 copy-start.5
  103.2 0.9 copy-start.7
  104.1 0.8 copy-start.9
  104.8 0.9 copy-start.11
  105.8 10.8 %copy-start.3 = (bf16[2,2,4,128,512]{4,3,2,1,0:T(8,128)(2,1)S(1)}, bf16[2,2,4,128,512]{4,3,2,1,0:T(8,128)(2,1)}, u32[]{:S(2)}) copy-start(bf16[2,2,4,128,512]{4,3,2,1,0:T(8,128)(2,1)} %copy-done.2) | copy-start | bytes 6291460
  105.8 10.8 %copy-start.8 = (f32[8192]{0:T(1024)S(1)}, f32[8192]{0:T(1024)}, u32[]{:S(2)}) copy-start(f32[8192]{0:T(1024)} %param.14) | copy-start | bytes 98308
  114.7 1.9 %copy-start.1 = (bf16[256,8192]{1,0:T(8,128)(2,1)}, bf16[256,8192]{1,0:T(8,128)(2,1)S(1)}, u32[]{:S(2)}) copy-start(bf16[256,8192]{1,0:T(8,128)(2,1)S(1)} %diag.1.partial) | copy-start | bytes 12582916

commit v3 on v2

--- a/solution.py
+++ b/solution.py
@@ -2,6 +2,7 @@
 
 import jax
 import jax.numpy as jnp
+import numpy as np
 from jax import lax
 from jax.experimental import pallas as pl
 from jax.experimental.pallas import tpu as pltpu
@@ -26,6 +27,30 @@
     high = value.astype(BF16)
     low = (value - high.astype(F32)).astype(BF16)
     return high, low
+
+
+def prepare_kernel(decay, step, skip, factor, grown, cum_rows, shifted, skips):
+    rows, heads = decay.shape
+    row_index = lax.broadcasted_iota(jnp.int32, (rows, rows), 0)
+    col_index = lax.broadcasted_iota(jnp.int32, (rows, rows), 1)
+    lower = jnp.where(row_index >= col_index, 1.0, 0.0).astype(F32)
+    cum = jnp.dot(
+        lower, jnp.log2(decay[...]), precision=lax.Precision.HIGHEST, preferred_element_type=F32
+    )
+    shifted[...] = (cum - jnp.log2(step[...])).T
+    per_group = heads // GROUPS
+
+    def doubled(value, out):
+        high, low = split_bf16(value)
+        for group in range(GROUPS):
+            at = slice(group * per_group, (group + 1) * per_group)
+            out[group] = jnp.concatenate([high[:, at], low[:, at]], axis=1)
+
+    doubled(jnp.exp2(cum[rows - 1 :] - cum) * step[...], factor)
+    doubled(jnp.exp2(cum), grown)
+    doubled(jnp.broadcast_to(skip[...], (16, heads)), skips)
+    for group in range(GROUPS):
+        cum_rows[group] = cum[:, group * per_group : (group + 1) * per_group]
 
 
 def conv_columns(x_ref, early_ref, weight_ref, out_ref, padded, rows):
@@ -45,7 +70,8 @@
 
 
 def conv_kernel(
-    xv, xb, xc, ev, eb, ec, wv, wb, wc, factor, expand, act_v, act_b, act_c, state, padded
+    xv, xb, xc, ev, eb, ec, wv, wb, wc, factor, grown, cum_rows, shifted, skips, expand,
+    act_c, state, decays, partial, padded, act_v, act_b
 ):
     rows = xv.shape[0]
     conv_columns(xv, ev, wv, act_v, padded, rows)
@@ -59,9 +85,12 @@
         wide = jnp.dot(factor[0], expand[:, at], preferred_element_type=F32)
         scaled = (act_v[:, at].astype(F32) * wide).astype(BF16)
         state[dest % 2, dest // 2 % 2, dest // 4] = jnp.dot(b_turned, scaled, preferred_element_type=F32).astype(BF16)
-
-
-def diag_kernel(act_v, act_b, act_c, cum_rows, shifted, skip, partial):
+        lasting = jnp.dot(grown[0, rows - 16 :], expand[:, at], preferred_element_type=F32)
+        decays[dest % 2, dest // 2 % 2, dest // 4] = lasting[15:16]
+    diag_part(act_v, act_b, act_c, cum_rows, shifted, skips, expand, partial)
+
+
+def diag_part(act_v, act_b, act_c, cum_rows, shifted, skips, expand, partial):
     rows = act_v.shape[0]
     half = rows // 2
     heads = cum_rows.shape[2]
@@ -89,7 +118,7 @@
             tops.append(jnp.dot(w_top, values[:half], preferred_element_type=F32))
             w_low = jnp.concatenate([w_left, w_right], axis=1)
             lows.append(jnp.dot(w_low, values, preferred_element_type=F32))
-        gain = skip[:, at]
+        gain = jnp.dot(skips[0], expand[:, at], preferred_element_type=F32)[0:1]
         wide = values.astype(F32)
         partial[:half, at] = (
             jnp.where(first_lanes, tops[0], tops[1]) + gain * wide[:half]
@@ -102,8 +131,10 @@
 def scan_kernel(
     planes, own, decays, start, incoming, final,
     cores, sent, kept, chips, plane_out, plane_in, enter, entered, back, mixed, handed,
+    core_rates, chip_rate_out, chip_rates, plane_rate_out, plane_rates,
     core_send, core_recv, chip_send, chip_recv, out_send, out_recv,
-    in_send, in_recv, back_send, back_recv, hand_send, hand_recv,
+    in_send, in_recv, back_send, back_recv, rate_send, rate_recv,
+    hand_send, hand_recv, few_send, few_recv,
 ):
     position = lax.axis_index("ctx")
     z, y, c = position // 4, (position // 2) % 2, position % 2
@@ -129,6 +160,11 @@
     pl.semaphore_wait(barrier, len(friends))
 
     pending = []
+    core_rate = copy(
+        decays.at[1 - c], core_rates, few_send.at[0], few_recv.at[0], core_peer
+    )
+    core_rate.start()
+    pending.append(core_rate)
     sides = (1 - y, y)
     swaps = []
     for turn, side in enumerate(sides):
@@ -145,8 +181,15 @@
 
     def chip_state(side, plane):
         earlier, later = core_states(side, plane)
-        return decays[side * planes + plane] * earlier + later
-
+        rate = jnp.where(first_core, core_rates[side, plane], decays[c, side, plane])
+        return rate * earlier + later
+
+    core_rate.wait_recv()
+    for plane in range(planes):
+        chip_rate_out[plane] = decays[c, 1 - y, plane] * core_rates[1 - y, plane]
+    chip_rate = copy(chip_rate_out, chip_rates, few_send.at[1], few_recv.at[1], chip_peer)
+    chip_rate.start()
+    pending.append(chip_rate)
     swaps[0].wait_recv()
     chip_copies = {}
     for step in order:
@@ -165,12 +208,31 @@
         here, there = kept[plane].astype(F32), chips[plane].astype(F32)
         return jnp.where(first_chip, here, there), jnp.where(first_chip, there, here)
 
-    out_copies = {}
+    def chip_rate_pair(plane):
+        here = decays[c, y, plane] * core_rates[y, plane]
+        there = chip_rates[plane]
+        return jnp.where(first_chip, here, there), jnp.where(first_chip, there, here)
+
+    chip_rate.wait_recv()
+    out_copies, rate_copies = {}, {}
+    for step in order:
+        plane = away[step]
+        earlier, later = chip_rate_pair(plane)
+        if step == 0:
+            plane_rates[plane] = earlier * later
+        else:
+            plane_rate_out[plane] = earlier * later
+            rate_copies[step] = copy(
+                plane_rate_out.at[plane], plane_rates.at[z], rate_send.at[step],
+                rate_recv.at[step], plane * 4 + y * 2 + c,
+            )
+            rate_copies[step].start()
+            pending.append(rate_copies[step])
     for step in order:
         plane = away[step]
         chip_copies[step].wait_recv()
         earlier, later = chip_states(plane)
-        both = (decays[4 * planes + plane] * earlier + later).astype(BF16)
+        both = (chip_rate_pair(plane)[1] * earlier + later).astype(BF16)
         if step == 0:
             plane_in[plane] = both
         else:
@@ -183,11 +245,12 @@
             pending.append(out_copies[step])
     for step in range(1, planes):
         out_copies[step].wait_recv()
+        rate_copies[step].wait_recv()
 
     now = start[...]
     for plane in range(planes):
         enter[plane] = now.astype(BF16)
-        now = decays[6 * planes + plane] * now + plane_in[plane].astype(F32)
+        now = plane_rates[plane] * now + plane_in[plane].astype(F32)
     final[...] = now
     in_copies = {}
     for step in range(1, planes):
@@ -203,7 +266,8 @@
 
     def to_cores(side, plane, state, slot):
         earlier, _ = core_states(side, plane)
-        later = decays[2 * planes + side * planes + plane] * state + earlier
+        rate = jnp.where(first_core, decays[c, side, plane], core_rates[side, plane])
+        later = rate * state + earlier
         incoming[c, side, plane] = jnp.where(first_core, state, later).astype(BF16)
         handed[side, plane] = jnp.where(first_core, later, state).astype(BF16)
         hand = copy(
@@ -223,7 +287,7 @@
             in_copies[step].wait_recv()
             state = entered[plane].astype(F32)
         earlier, _ = chip_states(plane)
-        later = decays[5 * planes + plane] * state + earlier
+        later = chip_rate_pair(plane)[0] * state + earlier
         back[plane] = jnp.where(first_chip, later, state).astype(BF16)
         back_copies[step] = copy(
             back.at[plane], mixed.at[plane], back_send.at[step], back_recv.at[step], chip_peer
@@ -278,37 +342,24 @@
     earlier = jnp.where(position == 0, conv_carry, received).astype(F32)
     earlier = jnp.pad(earlier, ((8 - (taps - 1), 0), (0, 0)))
 
-    logs = jnp.log2(decay)
-    lower = jnp.tril(jnp.ones((rows, rows), F32))
-    cum = jnp.dot(lower, logs, precision=lax.Precision.HIGHEST)
-    total = cum[-1]
-
-    def by_group(value):
-        return value.reshape(rows, GROUPS, -1).transpose(1, 0, 2)
-
-    def doubled(value):
-        high, low = split_bf16(by_group(value))
-        return jnp.concatenate([high, low], axis=2)
-
-    factor = doubled(jnp.exp2(total - cum) * step_size)
-    grown = doubled(jnp.exp2(cum))
-    shifted = (cum - jnp.log2(step_size)).T
-    spread = jnp.repeat(jnp.eye(per_group, dtype=BF16), P_SIZE, axis=1)
-    expand = jnp.concatenate([spread, spread], axis=0)
-
+    vmem = pl.BlockSpec(memory_space=pltpu.VMEM)
+    pairs = jax.ShapeDtypeStruct((GROUPS, rows, 2 * per_group), BF16)
+    factor, grown, cum_rows, shifted, skips = pl.pallas_call(
+        prepare_kernel,
+        in_specs=[vmem] * 3,
+        out_specs=[vmem] * 5,
+        out_shape=[
+            pairs,
+            pairs,
+            jax.ShapeDtypeStruct((GROUPS, rows, per_group), F32),
+            jax.ShapeDtypeStruct((heads, rows), F32),
+            jax.ShapeDtypeStruct((GROUPS, 16, 2 * per_group), BF16),
+        ],
+        name="prepare",
+    )(decay, step_size, skip_gain[None])
+    spread = np.repeat(np.eye(per_group, dtype=np.float32), P_SIZE, axis=1)
+    expand = jnp.asarray(np.concatenate([spread, spread], axis=0), BF16)
     planes = count // 4
-    at_z, at_y, at_c = position // 4, (position // 2) % 2, position % 2
-    every = lax.all_gather(total, "ctx").reshape(planes, 2, 2, planes, 2, 2, head_share)
-    every = every[:, :, :, :, :, at_c].transpose(0, 1, 2, 4, 3, 5)
-    plane_now = every[at_z]
-    pieces = [
-        plane_now[at_y, 1].reshape(2 * planes, head_share),
-        plane_now[at_y, 0].reshape(2 * planes, head_share),
-        plane_now[1].sum(0)[at_y],
-        plane_now[0].sum(0)[at_y],
-        every.sum((1, 2))[:, at_y, at_z],
-    ]
-    decays = jnp.repeat(jnp.exp2(jnp.concatenate(pieces, axis=0)), P_SIZE, axis=1)[:, None, :]
 
     def wide(height):
         return pl.BlockSpec((height, width), lambda g: (0, g))
@@ -322,48 +373,37 @@
     whole_expand = pl.BlockSpec((2 * per_group, width), lambda g: (0, 0))
     piece = pl.BlockSpec((2, 2, dests // 4, N, share), lambda g: (0, 0, g, 0, 0))
     b_first, c_first = inner // N, inner // N + GROUPS
-    act_v, act_b, act_c, own = pl.pallas_call(
+    rate = pl.BlockSpec((2, 2, dests // 4, 1, share), lambda g: (0, 0, g, 0, 0))
+    act_c, own, decays, partial = pl.pallas_call(
         conv_kernel,
         grid=(GROUPS,),
         in_specs=[
             wide(rows), thin(rows, b_first), thin(rows, c_first),
             wide(8), thin(8, b_first), thin(8, c_first),
             wide(taps), thin(taps, b_first), thin(taps, c_first),
-            per(rows, 2 * per_group), whole_expand,
-        ],
-        out_specs=[wide(rows), thin(rows, 0), thin(rows, 0), piece],
+            per(rows, 2 * per_group), per(rows, 2 * per_group), per(rows, per_group),
+            pl.BlockSpec((per_group, rows), lambda g: (g, 0)), per(16, 2 * per_group),
+            whole_expand,
+        ],
+        out_specs=[thin(rows, 0), piece, rate, wide(rows)],
         out_shape=[
-            jax.ShapeDtypeStruct((rows, inner), BF16),
-            jax.ShapeDtypeStruct((rows, GROUPS * N), BF16),
             jax.ShapeDtypeStruct((rows, GROUPS * N), BF16),
             jax.ShapeDtypeStruct((2, 2, planes, N, share), BF16),
-        ],
-        scratch_shapes=[pltpu.VMEM((8 + rows, LANES), F32)],
+            jax.ShapeDtypeStruct((2, 2, planes, 1, share), F32),
+            jax.ShapeDtypeStruct((rows, inner), BF16),
+        ],
+        scratch_shapes=[
+            pltpu.VMEM((8 + rows, LANES), F32),
+            pltpu.VMEM((rows, width), BF16),
+            pltpu.VMEM((rows, N), BF16),
+        ],
         compiler_params=params(),
         name="conv_state",
-    )(xbc, xbc, xbc, earlier, earlier, earlier, conv_weight, conv_weight, conv_weight, factor, expand)
-
-    partial = pl.pallas_call(
-        diag_kernel,
-        grid=(GROUPS,),
-        in_specs=[
-            wide(rows), thin(rows, 0), thin(rows, 0), per(rows, per_group),
-            pl.BlockSpec((per_group, rows), lambda g: (g, 0)), wide(1),
-        ],
-        out_specs=wide(rows),
-        out_shape=jax.ShapeDtypeStruct((rows, inner), BF16),
-        compiler_params=params(),
-        cost_estimate=pl.CostEstimate(
-            flops=heads * rows * rows * P_SIZE * 16,
-            bytes_accessed=rows * inner * 4,
-            transcendentals=heads * rows * rows,
-        ),
-        name="diag",
-    )(act_v, act_b, act_c, by_group(cum), shifted, jnp.repeat(skip_gain, P_SIZE)[None])
+    )(xbc, xbc, xbc, earlier, earlier, earlier, conv_weight, conv_weight, conv_weight, factor, grown,
+      cum_rows, shifted, skips, expand)
 
     start = lax.dynamic_slice_in_dim(init_state, position * head_share, head_share, 0)
     start = start.astype(F32).reshape(share, N).T
-    vmem = pl.BlockSpec(memory_space=pltpu.VMEM)
     line = pltpu.VMEM((planes, N, share), BF16)
     square = pltpu.VMEM((2, planes, N, share), BF16)
     turns = pltpu.SemaphoreType.DMA((planes,))
@@ -376,8 +416,9 @@
             jax.ShapeDtypeStruct((N, share), F32),
         ],
         scratch_shapes=[square] + [line] * 9 + [square]
-        + [pltpu.SemaphoreType.DMA((2,))] * 2 + [turns] * 8
-        + [pltpu.SemaphoreType.DMA((2 * planes,))] * 2,
+        + [pltpu.VMEM((2, planes, 1, share), F32)] + [pltpu.VMEM((planes, 1, share), F32)] * 4
+        + [pltpu.SemaphoreType.DMA((2,))] * 2 + [turns] * 10
+        + [pltpu.SemaphoreType.DMA((2 * planes,))] * 2 + [pltpu.SemaphoreType.DMA((2,))] * 2,
         compiler_params=pltpu.CompilerParams(
             collective_id=0, has_side_effects=True, vmem_limit_bytes=VMEM_LIMIT
         ),

time: 124 us -> 88 us (0.71)
  the two profiles are of different devices: /device:TPU:17 before, /device:TPU:27 now
where the time goes in v3:
time: 88 us; the launch traced here: 87.5 us
  Pallas kernels  73.3 us (83%)
  local copies, waits for them, and re-layouts  9.57 us (11%)
  starting transfers between devices  3.71 us (4%)
    pallas_call x1, Pallas kernels, shards(): pl.pallas_call(functools.partial(scan_kernel, planes), in_specs=[vmem] *...  44.1 us
    pallas_call x1, Pallas kernels, shards(): pl.pallas_call(conv_kernel, grid=(GROUPS,), in_specs=[wide(rows), thin(ro...  19.8 us
    unnamed x24, local copies, waits for them, and re-layouts  7.49 us
    pallas_call x1, Pallas kernels, shards(): pl.pallas_call(finish_kernel, grid=(GROUPS,), in_specs=[wide(rows), thin(...  6.77 us
    ppermute x1, starting transfers between devices, shards(): received = lax.ppermute(edge, 'ctx', [(s, s + 1) for s in range(count - 1)])  3.71 us
    pallas_call x1, Pallas kernels, shards(): pl.pallas_call(prepare_kernel, in_specs=[vmem] * 3, out_specs=[vmem] * 5,...  2.64 us
  transfers between devices with their start and end apart: 1, of which 0 were waited for; matrix products, arithmetic and copies ran while one was open for 0% of the time, Pallas kernels for 3%

profile of v3, /device:TPU:27, one launch (start us, length us, event | category | flops | bytes accessed | tf_op | source)
XLA Modules:
  0.0 87.5 jit_solution(13640426916436849720)
XLA Ops:
  0.6 0.0 copy-start
  0.6 0.0 copy-start.4
  0.7 0.0 copy-start.3
  0.7 1.1 %slice.3 = bf16[3,9216]{1,0:T(4,128)(2,1)S(1)} slice(bf16[256,9216]{1,0:T(8,128)(2,1)} %xc.1), slice={[253:256], [0:9216]} | slice | bytes 110592 | tf_op jit(solution)/shard_map/slice | solution.py:340
  1.8 3.7 %collective-permute-start = (bf16[3,9216]{1,0:T(4,128)(2,1)S(1)}, bf16[3,9216]{1,0:T(4,128)(2,1)S(1)}, u32[]{:S(2)}, u32[]{:S(2)}) collective-permute-start(bf16[3,9216]{1,0:T(4,128)(2,1)S(1)} %slice.3), channel_id=1, source_target_pairs={{0,1},{1,2},{2,3},{3,4},{4,5},{5,6},{6,7},{7,8},{8,9},{9,10},{10,1... | collective-permute-start | bytes 165896 | tf_op jit(solution)/shard_map/ppermute | solution.py:341
  5.5 0.0 copy-done
  5.6 0.1 copy.13
  5.7 2.6 %prepare.1 = (bf16[4,256,64]{2,1,0:T(8,128)(2,1)}, bf16[4,256,64]{2,1,0:T(8,128)(2,1)}, f32[4,256,32]{2,1,0:T(8,128)}, f32[128,256]{1,0:T(8,128)}, bf16[4,16,64]{2,1,0:T(8,128)(2,1)}) custom-call(f32[256,128]{1,0:T(8,128)} %decay.1, f32[256,128]{1,0:T(8,128)} %step.1, f32[1,128]{1,0:T(1,128)} %bitcast.12), custom_call_target="tpu_custom_call" | custom-call | tf_op jit(solution)/shard_map/prepare/pallas_call | solution.py:347
  8.3 0.0 collective-permute-done
  8.5 0.0 copy-done.4
  8.5 0.0 copy-done.3
  8.5 0.0 copy-start.5
  8.5 0.9 %copy-done.5 = bf16[4,256,64]{2,1,0:T(8,128)(2,1)S(1)} copy-done((bf16[4,256,64]{2,1,0:T(8,128)(2,1)S(1)}, bf16[4,256,64]{2,1,0:T(8,128)(2,1)}, u32[]{:S(2)}) %copy-start.5) | copy-done | bytes 131096
  9.4 0.0 copy-start.7
  9.4 1.0 %copy-done.7 = f32[4,256,32]{2,1,0:T(8,128)S(1)} copy-done((f32[4,256,32]{2,1,0:T(8,128)S(1)}, f32[4,256,32]{2,1,0:T(8,128)}, u32[]{:S(2)}) %copy-start.7) | copy-done | bytes 131096
  10.5 0.0 copy-start.8
  10.5 0.9 %copy-done.8 = bf16[4,256,64]{2,1,0:T(8,128)(2,1)S(1)} copy-done((bf16[4,256,64]{2,1,0:T(8,128)(2,1)S(1)}, bf16[4,256,64]{2,1,0:T(8,128)(2,1)}, u32[]{:S(2)}) %copy-start.8) | copy-done | bytes 131096
  11.4 0.0 copy-start.9
  11.4 0.9 %copy-done.9 = f32[128,256]{1,0:T(8,128)S(1)} copy-done((f32[128,256]{1,0:T(8,128)S(1)}, f32[128,256]{1,0:T(8,128)}, u32[]{:S(2)}) %copy-start.9) | copy-done | bytes 131096
  12.3 0.0 copy-start.11
  12.3 0.7 copy-done.11
  13.0 19.8 %conv_state.1 = (bf16[256,512]{1,0:T(8,128)(2,1)S(1)}, bf16[2,2,4,128,512]{4,3,2,1,0:T(8,128)(2,1)S(1)}, f32[2,2,4,1,512]{4,3,2,1,0:T(1,128)S(1)}, bf16[256,8192]{1,0:T(8,128)(2,1)}) custom-call(bf16[256,9216]{1,0:T(8,128)(2,1)} %xc.1, bf16[256,9216]{1,0:T(8,128)(2,1)} %xc.1, bf16[256,9216]{1,0:T(8,128)(2,1)} %xc.1, f32[8,9216]{1,0:T(8,128)S(1)} %pad_convert_fusion.ev.eb.ec, ...), custom_call_target="tpu_custom_call" | custom-call | tf_op jit(solution)/shard_map/conv_state/pallas_call | solution.py:377
  32.8 0.0 copy-start.6
  32.8 0.0 copy-start.10
  32.8 44.1 %scan_devices.1 = (bf16[2,2,4,128,512]{4,3,2,1,0:T(8,128)(2,1)S(1)}, f32[128,512]{1,0:T(8,128)S(1)}) custom-call(bf16[2,2,4,128,512]{4,3,2,1,0:T(8,128)(2,1)S(1)} %get-tuple-element.20.own, f32[2,2,4,1,512]{4,3,2,1,0:T(1,128)S(1)} %get-tuple-element.21.decays, f32[128,512]{1,0:T(8,128)S(1)} %bitcast.8), custom_call_target="tpu_custom_call" | custom-call | tf_op jit(solution)/shard_map/scan_devices/pallas_call | solution.py:410
  77.0 0.0 copy-start.1
  77.0 1.3 %copy-done.1 = bf16[2,2,4,128,512]{4,3,2,1,0:T(8,128)(2,1)} copy-done((bf16[2,2,4,128,512]{4,3,2,1,0:T(8,128)(2,1)}, bf16[2,2,4,128,512]{4,3,2,1,0:T(8,128)(2,1)S(1)}, u32[]{:S(2)}) %copy-start.1) | copy-done | bytes 2097176
  78.3 0.8 copy.14
  79.1 0.0 copy-done.6
  79.1 0.0 copy-done.10
  79.1 0.0 copy-start.2
  79.1 1.6 %copy-done.2 = bf16[2,2,4,128,512]{4,3,2,1,0:T(8,128)(2,1)S(1)} copy-done((bf16[2,2,4,128,512]{4,3,2,1,0:T(8,128)(2,1)S(1)}, bf16[2,2,4,128,512]{4,3,2,1,0:T(8,128)(2,1)}, u32[]{:S(2)}) %copy-start.2) | copy-done | bytes 2097176
  80.7 6.8 %finish.1 = bf16[256,8192]{1,0:T(8,128)(2,1)} custom-call(bf16[256,8192]{1,0:T(8,128)(2,1)} %get-tuple-element.18.partial, bf16[256,512]{1,0:T(8,128)(2,1)S(1)} %get-tuple-element.19.act_c, bf16[2,2,4,128,512]{4,3,2,1,0:T(8,128)(2,1)S(1)} %copy-done.2, bf16[4,256,64]{2,1,0:T(8,128)(2,1)S(1)} %copy-done.6, bf16[64,2048]{1,0:T(8,128)(2,1)S(1)} %copy-done.4, ...), custom_call_target="tpu_custom_call" | custom-call | tf_op jit(solution)/shard_map/finish/pallas_call | solution.py:429
  (4 shorter events, 0.1 us)
Async XLA Ops:
  0.6 4.9 %copy-start = (bf16[128,64,128]{2,1,0:T(8,128)(2,1)S(1)}, bf16[128,64,128]{2,1,0:T(8,128)(2,1)}, u32[]{:S(2)}) copy-start(bf16[128,64,128]{2,1,0:T(8,128)(2,1)} %param.16) | copy-start | bytes 6291460
  0.6 7.8 %copy-start.4 = (bf16[64,2048]{1,0:T(8,128)(2,1)S(1)}, bf16[64,2048]{1,0:T(8,128)(2,1)}, u32[]{:S(2)}) copy-start(bf16[64,2048]{1,0:T(8,128)(2,1)} %constant.15.clone.expand) | copy-start | bytes 786436
  0.7 7.8 %copy-start.3 = (f32[4,9216]{1,0:T(4,128)S(1)}, f32[4,9216]{1,0:T(4,128)}, u32[]{:S(2)}) copy-start(f32[4,9216]{1,0:T(4,128)} %wc.1) | copy-start | bytes 442372
  1.8 6.6 %collective-permute-start = (bf16[3,9216]{1,0:T(4,128)(2,1)S(1)}, bf16[3,9216]{1,0:T(4,128)(2,1)S(1)}, u32[]{:S(2)}, u32[]{:S(2)}) collective-permute-start(bf16[3,9216]{1,0:T(4,128)(2,1)S(1)} %slice.3), channel_id=1, source_target_pairs={{0,1},{1,2},{2,3},{3,4},{4,5},{5,6},{6,7},{7,8},{8,9},{9,10},{10,1... | collective-permute-start | bytes 165896 | tf_op jit(solution)/shard_map/ppermute | solution.py:341
  8.5 1.0 %copy-start.5 = (bf16[4,256,64]{2,1,0:T(8,128)(2,1)S(1)}, bf16[4,256,64]{2,1,0:T(8,128)(2,1)}, u32[]{:S(2)}) copy-start(bf16[4,256,64]{2,1,0:T(8,128)(2,1)} %get-tuple-element.14.grown) | copy-start | bytes 393220
  9.4 1.0 %copy-start.7 = (f32[4,256,32]{2,1,0:T(8,128)S(1)}, f32[4,256,32]{2,1,0:T(8,128)}, u32[]{:S(2)}) copy-start(f32[4,256,32]{2,1,0:T(8,128)} %get-tuple-element.15.cum_rows) | copy-start | bytes 393220
  10.5 0.9 %copy-start.8 = (bf16[4,256,64]{2,1,0:T(8,128)(2,1)S(1)}, bf16[4,256,64]{2,1,0:T(8,128)(2,1)}, u32[]{:S(2)}) copy-start(bf16[4,256,64]{2,1,0:T(8,128)(2,1)} %get-tuple-element.13.factor) | copy-start | bytes 393220
  11.4 0.9 %copy-start.9 = (f32[128,256]{1,0:T(8,128)S(1)}, f32[128,256]{1,0:T(8,128)}, u32[]{:S(2)}) copy-start(f32[128,256]{1,0:T(8,128)} %get-tuple-element.16.shifted) | copy-start | bytes 393220
  12.3 0.7 copy-start.11
  32.8 46.3 %copy-start.6 = (bf16[4,256,64]{2,1,0:T(8,128)(2,1)S(1)}, bf16[4,256,64]{2,1,0:T(8,128)(2,1)}, u32[]{:S(2)}) copy-start(bf16[4,256,64]{2,1,0:T(8,128)(2,1)} %get-tuple-element.14.grown) | copy-start | bytes 393220
  32.8 46.3 %copy-start.10 = (f32[8192]{0:T(1024)S(1)}, f32[8192]{0:T(1024)}, u32[]{:S(2)}) copy-start(f32[8192]{0:T(1024)} %param.15) | copy-start | bytes 98308
  77.0 1.3 %copy-start.1 = (bf16[2,2,4,128,512]{4,3,2,1,0:T(8,128)(2,1)}, bf16[2,2,4,128,512]{4,3,2,1,0:T(8,128)(2,1)S(1)}, u32[]{:S(2)}) copy-start(bf16[2,2,4,128,512]{4,3,2,1,0:T(8,128)(2,1)S(1)} %get-tuple-element.22.incoming) | copy-start | bytes 6291460
  79.1 1.6 %copy-start.2 = (bf16[2,2,4,128,512]{4,3,2,1,0:T(8,128)(2,1)S(1)}, bf16[2,2,4,128,512]{4,3,2,1,0:T(8,128)(2,1)}, u32[]{:S(2)}) copy-start(bf16[2,2,4,128,512]{4,3,2,1,0:T(8,128)(2,1)} %copy-done.1) | copy-start | bytes 6291460

commit v4 on v3

--- a/solution.py
+++ b/solution.py
@@ -29,7 +29,7 @@
     return high, low
 
 
-def prepare_kernel(decay, step, skip, factor, grown, cum_rows, shifted, skips):
+def prepare(decay, step, skip, factor, grown, cum_rows, shifted, skips):
     rows, heads = decay.shape
     row_index = lax.broadcasted_iota(jnp.int32, (rows, rows), 0)
     col_index = lax.broadcasted_iota(jnp.int32, (rows, rows), 1)
@@ -37,8 +37,8 @@
     cum = jnp.dot(
         lower, jnp.log2(decay[...]), precision=lax.Precision.HIGHEST, preferred_element_type=F32
     )
-    shifted[...] = (cum - jnp.log2(step[...])).T
     per_group = heads // GROUPS
+    shifted[...] = (cum - jnp.log2(step[...])).T.reshape(GROUPS, per_group, rows)
 
     def doubled(value, out):
         high, low = split_bf16(value)
@@ -70,9 +70,19 @@
 
 
 def conv_kernel(
-    xv, xb, xc, ev, eb, ec, wv, wb, wc, factor, grown, cum_rows, shifted, skips, expand,
-    act_c, state, decays, partial, padded, act_v, act_b
+    xv, xb, xc, ev, eb, ec, wv, wb, wc, decay, step, skip, expand,
+    act_c, state, decays, partial, all_grown, padded, act_v, act_b,
+    all_factor, all_cum, all_shifted, all_skips
 ):
+    group = pl.program_id(0)
+
+    @pl.when(group == 0)
+    def _():
+        prepare(decay, step, skip, all_factor, all_grown, all_cum, all_shifted, all_skips)
+
+    own = pl.ds(group, 1)
+    factor, grown, cum_rows = all_factor.at[own], all_grown.at[own], all_cum.at[own]
+    shifted, skips = all_shifted.at[own], all_skips.at[own]
     rows = xv.shape[0]
     conv_columns(xv, ev, wv, act_v, padded, rows)
     conv_columns(xb, eb, wb, act_b, padded, rows)
@@ -108,7 +118,7 @@
         tops, lows = [], []
         for head in (2 * pair, 2 * pair + 1):
             own = cum[:, head : head + 1]
-            other = shifted[head : head + 1, :]
+            other = shifted[0, head : head + 1, :]
             top = jnp.where(lower, own[:half] - other[:, :half], -1e30)
             w_top = (scores[:half, :half] * jnp.exp2(top)).astype(BF16)
             left = own[half:] - other[:, :half]
@@ -343,20 +353,6 @@
     earlier = jnp.pad(earlier, ((8 - (taps - 1), 0), (0, 0)))
 
     vmem = pl.BlockSpec(memory_space=pltpu.VMEM)
-    pairs = jax.ShapeDtypeStruct((GROUPS, rows, 2 * per_group), BF16)
-    factor, grown, cum_rows, shifted, skips = pl.pallas_call(
-        prepare_kernel,
-        in_specs=[vmem] * 3,
-        out_specs=[vmem] * 5,
-        out_shape=[
-            pairs,
-            pairs,
-            jax.ShapeDtypeStruct((GROUPS, rows, per_group), F32),
-            jax.ShapeDtypeStruct((heads, rows), F32),
-            jax.ShapeDtypeStruct((GROUPS, 16, 2 * per_group), BF16),
-        ],
-        name="prepare",
-    )(decay, step_size, skip_gain[None])
     spread = np.repeat(np.eye(per_group, dtype=np.float32), P_SIZE, axis=1)
     expand = jnp.asarray(np.concatenate([spread, spread], axis=0), BF16)
     planes = count // 4
@@ -370,37 +366,44 @@
     def per(*shape):
         return pl.BlockSpec((1,) + shape, lambda g: (g, 0, 0))
 
+    def fixed(*shape):
+        return pl.BlockSpec(shape, lambda g: (0,) * len(shape))
+
+    pairs = (GROUPS, rows, 2 * per_group)
     whole_expand = pl.BlockSpec((2 * per_group, width), lambda g: (0, 0))
     piece = pl.BlockSpec((2, 2, dests // 4, N, share), lambda g: (0, 0, g, 0, 0))
     b_first, c_first = inner // N, inner // N + GROUPS
     rate = pl.BlockSpec((2, 2, dests // 4, 1, share), lambda g: (0, 0, g, 0, 0))
-    act_c, own, decays, partial = pl.pallas_call(
+    act_c, own, decays, partial, grown = pl.pallas_call(
         conv_kernel,
         grid=(GROUPS,),
         in_specs=[
             wide(rows), thin(rows, b_first), thin(rows, c_first),
             wide(8), thin(8, b_first), thin(8, c_first),
             wide(taps), thin(taps, b_first), thin(taps, c_first),
-            per(rows, 2 * per_group), per(rows, 2 * per_group), per(rows, per_group),
-            pl.BlockSpec((per_group, rows), lambda g: (g, 0)), per(16, 2 * per_group),
-            whole_expand,
+            fixed(rows, heads), fixed(rows, heads), fixed(1, heads), whole_expand,
         ],
-        out_specs=[thin(rows, 0), piece, rate, wide(rows)],
+        out_specs=[thin(rows, 0), piece, rate, wide(rows), fixed(*pairs)],
         out_shape=[
             jax.ShapeDtypeStruct((rows, GROUPS * N), BF16),
             jax.ShapeDtypeStruct((2, 2, planes, N, share), BF16),
             jax.ShapeDtypeStruct((2, 2, planes, 1, share), F32),
             jax.ShapeDtypeStruct((rows, inner), BF16),
+            jax.ShapeDtypeStruct(pairs, BF16),
         ],
         scratch_shapes=[
             pltpu.VMEM((8 + rows, LANES), F32),
             pltpu.VMEM((rows, width), BF16),
             pltpu.VMEM((rows, N), BF16),
+            pltpu.VMEM(pairs, BF16),
+            pltpu.VMEM((GROUPS, rows, per_group), F32),
+            pltpu.VMEM((GROUPS, per_group, rows), F32),
+            pltpu.VMEM((GROUPS, 16, 2 * per_group), BF16),
         ],
         compiler_params=params(),
         name="conv_state",
-    )(xbc, xbc, xbc, earlier, earlier, earlier, conv_weight, conv_weight, conv_weight, factor, grown,
-      cum_rows, shifted, skips, expand)
+    )(xbc, xbc, xbc, earlier, earlier, earlier, conv_weight, conv_weight, conv_weight, decay,
+      step_size, skip_gain[None], expand)
 
     start = lax.dynamic_slice_in_dim(init_state, position * head_share, head_share, 0)
     start = start.astype(F32).reshape(share, N).T

time: 88 us -> 87.7 us (level)
  the two profiles are of different devices: /device:TPU:27 before, /device:TPU:17 now
where the time goes in v4:
time: 87.7 us; the launch traced here: 87.3 us
  Pallas kernels  73.2 us (83%)
  local copies, waits for them, and re-layouts  8.37 us (10%)
  starting transfers between devices  3.71 us (4%)
  waiting for transfers between devices  1.17 us (1%)
    pallas_call x1, Pallas kernels, shards(): pl.pallas_call(functools.partial(scan_kernel, planes), in_specs=[vmem] *...  45.6 us
    pallas_call x1, Pallas kernels, shards(): pl.pallas_call(conv_kernel, grid=(GROUPS,), in_specs=[wide(rows), thin(ro...  20.8 us
    pallas_call x1, Pallas kernels, shards(): pl.pallas_call(finish_kernel, grid=(GROUPS,), in_specs=[wide(rows), thin(...  6.77 us
    unnamed x18, local copies, waits for them, and re-layouts  6.29 us
    ppermute x1, starting transfers between devices, shards(): received = lax.ppermute(edge, 'ctx', [(s, s + 1) for s in range(count - 1)])  3.71 us
  transfers between devices with their start and end apart: 1, of which 1 were waited for; matrix products, arithmetic and copies ran while one was open for 0% of the time, Pallas kernels for 0%

profile of v4, /device:TPU:17, one launch (start us, length us, event | category | flops | bytes accessed | tf_op | source)
XLA Modules:
  0.0 87.3 jit_solution(14640866350474753852)
XLA Ops:
  0.6 0.0 copy-start
  0.6 0.0 copy-start.4
  0.7 1.1 %slice.3 = bf16[3,9216]{1,0:T(4,128)(2,1)S(1)} slice(bf16[256,9216]{1,0:T(8,128)(2,1)} %xc.1), slice={[253:256], [0:9216]} | slice | bytes 110592 | tf_op jit(solution)/shard_map/slice | solution.py:350
  1.8 3.7 %collective-permute-start = (bf16[3,9216]{1,0:T(4,128)(2,1)S(1)}, bf16[3,9216]{1,0:T(4,128)(2,1)S(1)}, u32[]{:S(2)}, u32[]{:S(2)}) collective-permute-start(bf16[3,9216]{1,0:T(4,128)(2,1)S(1)} %slice.3), channel_id=1, source_target_pairs={{0,1},{1,2},{2,3},{3,4},{4,5},{5,6},{6,7},{7,8},{8,9},{9,10},{10,1... | collective-permute-start | bytes 165896 | tf_op jit(solution)/shard_map/ppermute | solution.py:351
  5.5 0.0 copy-done
  5.6 0.1 copy.13
  5.7 1.2 %collective-permute-done = bf16[3,9216]{1,0:T(4,128)(2,1)S(1)} collective-permute-done((bf16[3,9216]{1,0:T(4,128)(2,1)S(1)}, bf16[3,9216]{1,0:T(4,128)(2,1)S(1)}, u32[]{:S(2)}, u32[]{:S(2)}) %collective-permute-start) | collective-permute-done | bytes 55328 | tf_op jit(solution)/shard_map/ppermute | solution.py:351
  7.0 0.0 copy-done.4
  7.0 0.0 copy-start.3
  7.0 0.9 %copy-done.3 = f32[4,9216]{1,0:T(4,128)S(1)} copy-done((f32[4,9216]{1,0:T(4,128)S(1)}, f32[4,9216]{1,0:T(4,128)}, u32[]{:S(2)}) %copy-start.3) | copy-done | bytes 147480
  7.9 0.0 copy-start.5
  7.9 0.9 %copy-done.5 = f32[256,128]{1,0:T(8,128)S(1)} copy-done((f32[256,128]{1,0:T(8,128)S(1)}, f32[256,128]{1,0:T(8,128)}, u32[]{:S(2)}) %copy-start.5) | copy-done | bytes 131096
  8.8 0.0 copy-start.6
  8.8 0.9 %copy-done.6 = f32[256,128]{1,0:T(8,128)S(1)} copy-done((f32[256,128]{1,0:T(8,128)S(1)}, f32[256,128]{1,0:T(8,128)}, u32[]{:S(2)}) %copy-start.6) | copy-done | bytes 131096
  9.7 0.0 copy-start.8
  9.7 0.7 copy-done.8
  10.4 20.8 %conv_state.1 = (bf16[256,512]{1,0:T(8,128)(2,1)S(1)}, bf16[2,2,4,128,512]{4,3,2,1,0:T(8,128)(2,1)S(1)}, f32[2,2,4,1,512]{4,3,2,1,0:T(1,128)S(1)}, bf16[256,8192]{1,0:T(8,128)(2,1)}, bf16[4,256,64]{2,1,0:T(8,128)(2,1)S(1)}) custom-call(bf16[256,9216]{1,0:T(8,128)(2,1)} %xc.1, bf16[256,9216]{1,0:T(8,128)(2,1)} %xc.1, bf16[256,9216]{1,0:T(8,128)(2,1)} %xc.1, ...), custom_call_target="tpu_custom_call" | custom-call | tf_op jit(solution)/shard_map/conv_state/pallas_call | solution.py:377
  31.2 0.0 copy-start.7
  31.2 45.6 %scan_devices.1 = (bf16[2,2,4,128,512]{4,3,2,1,0:T(8,128)(2,1)S(1)}, f32[128,512]{1,0:T(8,128)S(1)}) custom-call(bf16[2,2,4,128,512]{4,3,2,1,0:T(8,128)(2,1)S(1)} %get-tuple-element.11.own, f32[2,2,4,1,512]{4,3,2,1,0:T(1,128)S(1)} %get-tuple-element.12.decays, f32[128,512]{1,0:T(8,128)S(1)} %bitcast.8), custom_call_target="tpu_custom_call" | custom-call | tf_op jit(solution)/shard_map/scan_devices/pallas_call | solution.py:413
  76.8 0.0 copy-start.1
  76.8 1.3 %copy-done.1 = bf16[2,2,4,128,512]{4,3,2,1,0:T(8,128)(2,1)} copy-done((bf16[2,2,4,128,512]{4,3,2,1,0:T(8,128)(2,1)}, bf16[2,2,4,128,512]{4,3,2,1,0:T(8,128)(2,1)S(1)}, u32[]{:S(2)}) %copy-start.1) | copy-done | bytes 2097176
  78.1 0.8 copy.14
  78.9 0.0 copy-done.7
  78.9 0.0 copy-start.2
  78.9 1.6 %copy-done.2 = bf16[2,2,4,128,512]{4,3,2,1,0:T(8,128)(2,1)S(1)} copy-done((bf16[2,2,4,128,512]{4,3,2,1,0:T(8,128)(2,1)S(1)}, bf16[2,2,4,128,512]{4,3,2,1,0:T(8,128)(2,1)}, u32[]{:S(2)}) %copy-start.2) | copy-done | bytes 2097176
  80.5 6.8 %finish.1 = bf16[256,8192]{1,0:T(8,128)(2,1)} custom-call(bf16[256,8192]{1,0:T(8,128)(2,1)} %get-tuple-element.9.partial, bf16[256,512]{1,0:T(8,128)(2,1)S(1)} %get-tuple-element.10.act_c, bf16[2,2,4,128,512]{4,3,2,1,0:T(8,128)(2,1)S(1)} %copy-done.2, bf16[4,256,64]{2,1,0:T(8,128)(2,1)S(1)} %get-tuple-element.14.grown, bf16[64,2048]{1,0:T(8,128)(2,1)S(1)} %copy-done.4, ...), custom_call_target="tpu_custom_call" | custom-call | tf_op jit(solution)/shard_map/finish/pallas_call | solution.py:432
  (4 shorter events, 0.1 us)
Async XLA Ops:
  0.6 4.9 %copy-start = (bf16[128,64,128]{2,1,0:T(8,128)(2,1)S(1)}, bf16[128,64,128]{2,1,0:T(8,128)(2,1)}, u32[]{:S(2)}) copy-start(bf16[128,64,128]{2,1,0:T(8,128)(2,1)} %param.16) | copy-start | bytes 6291460
  0.6 6.3 %copy-start.4 = (bf16[64,2048]{1,0:T(8,128)(2,1)S(1)}, bf16[64,2048]{1,0:T(8,128)(2,1)}, u32[]{:S(2)}) copy-start(bf16[64,2048]{1,0:T(8,128)(2,1)} %constant.15.clone.expand) | copy-start | bytes 786436
  1.8 5.1 %collective-permute-start = (bf16[3,9216]{1,0:T(4,128)(2,1)S(1)}, bf16[3,9216]{1,0:T(4,128)(2,1)S(1)}, u32[]{:S(2)}, u32[]{:S(2)}) collective-permute-start(bf16[3,9216]{1,0:T(4,128)(2,1)S(1)} %slice.3), channel_id=1, source_target_pairs={{0,1},{1,2},{2,3},{3,4},{4,5},{5,6},{6,7},{7,8},{8,9},{9,10},{10,1... | collective-permute-start | bytes 165896 | tf_op jit(solution)/shard_map/ppermute | solution.py:351
  7.0 0.9 %copy-start.3 = (f32[4,9216]{1,0:T(4,128)S(1)}, f32[4,9216]{1,0:T(4,128)}, u32[]{:S(2)}) copy-start(f32[4,9216]{1,0:T(4,128)} %wc.1) | copy-start | bytes 442372
  7.9 0.9 %copy-start.5 = (f32[256,128]{1,0:T(8,128)S(1)}, f32[256,128]{1,0:T(8,128)}, u32[]{:S(2)}) copy-start(f32[256,128]{1,0:T(8,128)} %decay.1) | copy-start | bytes 393220
  8.8 0.9 %copy-start.6 = (f32[256,128]{1,0:T(8,128)S(1)}, f32[256,128]{1,0:T(8,128)}, u32[]{:S(2)}) copy-start(f32[256,128]{1,0:T(8,128)} %step.1) | copy-start | bytes 393220
  9.7 0.7 copy-start.8
  31.2 47.8 %copy-start.7 = (f32[8192]{0:T(1024)S(1)}, f32[8192]{0:T(1024)}, u32[]{:S(2)}) copy-start(f32[8192]{0:T(1024)} %param.15) | copy-start | bytes 98308
  76.8 1.3 %copy-start.1 = (bf16[2,2,4,128,512]{4,3,2,1,0:T(8,128)(2,1)}, bf16[2,2,4,128,512]{4,3,2,1,0:T(8,128)(2,1)S(1)}, u32[]{:S(2)}) copy-start(bf16[2,2,4,128,512]{4,3,2,1,0:T(8,128)(2,1)S(1)} %get-tuple-element.13.incoming) | copy-start | bytes 6291460
  78.9 1.6 %copy-start.2 = (bf16[2,2,4,128,512]{4,3,2,1,0:T(8,128)(2,1)S(1)}, bf16[2,2,4,128,512]{4,3,2,1,0:T(8,128)(2,1)}, u32[]{:S(2)}) copy-start(bf16[2,2,4,128,512]{4,3,2,1,0:T(8,128)(2,1)} %copy-done.1) | copy-start | bytes 6291460
